TPU v7x, 32 devices: a whole 2x2x4 slice. The times are simulated.
32 devices in a mesh: lat: 4 (over x, core), lon: 8 (over z, y).
Axes of the slice: x: 2, y: 2, z: 4, core: 2. Of those that a mesh axis runs over, the one named last changes fastest.
Arguments:
- fine_query: bfloat16 [96, 256, 512], P('lat', 'lon'), may hold values from -6 to 6
- fine_keyval: bfloat16 [96, 256, 1024], P('lat', 'lon'), may hold values from -6 to 6
- coarse_query: bfloat16 [24, 64, 512], P('lat', 'lon'), may hold values from -6 to 6
- coarse_keyval: bfloat16 [24, 64, 1024], P('lat', 'lon'), may hold values from -6 to 6
- out_weight: bfloat16 [512, 512], replicated, may hold values from -0.25 to 0.25
Outputs:
- output: bfloat16 [96, 256, 512], P('lat', 'lon')
All inputs are finite; a program needn't handle non-finite values.
Results may differ from a plain program's by a relative error of at most 0.0061.
Values may be sent and summed in bfloat16 or wider, within the bound.
No kernel may reach another device: no remote copies, remote signals or barrier semaphores. Data moves between devices by JAX's collectives and lax.ppermute only.
A program may use at most 64 MiB of HBM per device.

v0:
```python
import math

import jax
import jax.numpy as jnp
from jax import lax
from jax.sharding import PartitionSpec as P

HEADS = 8
RADIUS = 6


NEGATIVE = -1e30


def with_halo(block, sides, width):
    for axis, dim in sides:
        count = lax.axis_size(axis)
        forward = [(i, i + 1) for i in range(count - 1)]
        forward.append((count - 1, 0))
        backward = [(target, source) for source, target in forward]
        low = lax.ppermute(
            lax.slice_in_dim(block, block.shape[dim] - width, None, axis=dim), axis, forward
        )
        high = lax.ppermute(lax.slice_in_dim(block, 0, width, axis=dim), axis, backward)
        block = jnp.concatenate([low, block, high], axis=dim)
    return block


def window_allowed(tile_rows, tile_cols, radius, rows_valid):
    ext_rows = tile_rows + 2 * radius
    ext_cols = tile_cols + 2 * radius
    query_pos = jnp.arange(tile_rows * tile_cols, dtype=jnp.int32)
    key_pos = jnp.arange(ext_rows * ext_cols, dtype=jnp.int32)
    lat_gap = (key_pos // ext_cols)[None, :] - radius - (query_pos // tile_cols)[:, None]
    lon_gap = (key_pos % ext_cols)[None, :] - radius - (query_pos % tile_cols)[:, None]
    key_valid = jnp.repeat(rows_valid, ext_cols)
    return (jnp.abs(lat_gap) <= radius) & (jnp.abs(lon_gap) <= radius) & key_valid[None, :]


def rows_inside(tile_index, tile_rows, radius, total_rows):
    global_rows = (
        tile_index * tile_rows - radius + jnp.arange(tile_rows + 2 * radius, dtype=jnp.int32)
    )
    return (global_rows >= 0) & (global_rows < total_rows)


def attend(queries, keyval, allowed, head_count):
    length, channels = queries.shape
    head_dim = channels // head_count
    scaling_factor = 1.0 / math.sqrt(head_dim)
    head_group = math.gcd(head_count, max(1, 128 // head_dim))
    group_span = head_group * head_dim
    group_count = head_count // head_group

    def one_group(block, result):
        query_portion = lax.dynamic_slice_in_dim(
            queries, block * group_span, group_span, 1
        ).reshape(length, head_group, head_dim)
        key_portion = lax.dynamic_slice_in_dim(keyval, block * group_span, group_span, 1).reshape(
            -1, head_group, head_dim
        )
        value_portion = lax.dynamic_slice_in_dim(
            keyval, channels + block * group_span, group_span, 1
        ).reshape(-1, head_group, head_dim)
        logit_scores = (
            jnp.einsum(
                "mgd,ngd->gmn", query_portion, key_portion, preferred_element_type=jnp.float32
            )
            * scaling_factor
        )
        if allowed is not None:
            logit_scores = jnp.where(allowed[None, :, :], logit_scores, NEGATIVE)
        logit_scores = logit_scores - jnp.max(logit_scores, axis=-1, keepdims=True)
        raised = jnp.exp(logit_scores)
        softmax_weights = (raised / jnp.sum(raised, axis=-1, keepdims=True)).astype(jnp.bfloat16)
        blended_output = jnp.einsum(
            "gmn,ngd->mgd", softmax_weights, value_portion, preferred_element_type=jnp.float32
        )
        return lax.dynamic_update_slice_in_dim(
            result, blended_output.reshape(length, group_span), block * group_span, 1
        )

    return lax.fori_loop(0, group_count, one_group, jnp.zeros((length, channels), jnp.float32))


def upsample_table(fine_size):
    fine_index = jnp.arange(fine_size, dtype=jnp.int32)
    coarse_index = fine_index // 4
    offset = ((fine_index % 4).astype(jnp.float32) - 1.5) / 4.0
    columns = jnp.arange(fine_size // 4 + 2, dtype=jnp.int32)
    before = jnp.where(offset < 0, -offset, 0.0)
    after = jnp.where(offset > 0, offset, 0.0)
    centre = 1.0 - jnp.abs(offset)
    table = jnp.where(columns[None, :] == coarse_index[:, None], before[:, None], 0.0)
    table = table + jnp.where(columns[None, :] == coarse_index[:, None] + 1, centre[:, None], 0.0)
    table = table + jnp.where(columns[None, :] == coarse_index[:, None] + 2, after[:, None], 0.0)
    return table


def fold_poles(table, lat_index, lat_count):
    folded_top = table.at[:, 1].add(table[:, 0]).at[:, 0].set(0.0)
    table = jnp.where(lat_index == 0, folded_top, table)
    folded_bottom = table.at[:, -2].add(table[:, -1]).at[:, -1].set(0.0)
    return jnp.where(lat_index == lat_count - 1, folded_bottom, table)


def upsample(coarse, lat_table, lon_table):
    halfway = jnp.einsum(
        "ia,abc->ibc", lat_table, coarse.astype(jnp.float32), precision=lax.Precision.HIGHEST
    )
    return jnp.einsum("jb,ibc->ijc", lon_table, halfway, precision=lax.Precision.HIGHEST)


def fine_window_attention(fine_query, fine_extended, row_valid, radius):
    tile_rows, tile_cols, channels = fine_query.shape
    block_rows = 8
    block_cols = 16
    across = tile_cols // block_cols
    down = tile_rows // block_rows
    zero = jnp.zeros((), jnp.int32)

    def one_block(index):
        row_start = index // across * block_rows
        col_start = index % across * block_cols
        block_query = lax.dynamic_slice(
            fine_query, (row_start, col_start, zero), (block_rows, block_cols, channels)
        )
        block_keys = lax.dynamic_slice(
            fine_extended,
            (row_start, col_start, zero),
            (block_rows + 2 * radius, block_cols + 2 * radius, 2 * channels),
        )
        block_valid = lax.dynamic_slice_in_dim(row_valid, row_start, block_rows + 2 * radius, 0)
        allowed = window_allowed(block_rows, block_cols, radius, block_valid)
        blended_output = attend(
            block_query.reshape(-1, channels), block_keys.reshape(-1, 2 * channels), allowed, HEADS
        )
        return blended_output.astype(jnp.bfloat16).reshape(block_rows, block_cols, channels)

    blocks = lax.map(one_block, jnp.arange(down * across, dtype=jnp.int32))
    blocks = blocks.reshape(down, across, block_rows, block_cols, channels).transpose(0, 2, 1, 3, 4)
    return blocks.reshape(tile_rows * tile_cols, channels)


def shards(fine_query, fine_keyval, coarse_query, coarse_keyval, out_weight):
    tile_rows, tile_cols, channels = fine_query.shape
    coarse_rows = coarse_query.shape[0]
    coarse_cols = coarse_query.shape[1]
    radius = RADIUS
    lat_index = lax.axis_index("lat")
    lat_count = lax.axis_size("lat")
    fine_extended = with_halo(fine_keyval, (("lat", 0), ("lon", 1)), radius)
    coarse_extended = with_halo(coarse_keyval, (("lat", 0), ("lon", 1)), radius)
    coarse_allowed = window_allowed(
        coarse_rows,
        coarse_cols,
        radius,
        rows_inside(lat_index, coarse_rows, radius, coarse_rows * lat_count),
    )
    coarse_att = attend(
        coarse_query.reshape(-1, channels),
        coarse_extended.reshape(-1, 2 * channels),
        coarse_allowed,
        HEADS,
    )
    coarse_att = coarse_att.astype(jnp.bfloat16).reshape(coarse_rows, coarse_cols, channels)
    cycle_att = with_halo(coarse_att, (("lat", 0), ("lon", 1)), 1)
    row_valid = rows_inside(lat_index, tile_rows, radius, tile_rows * lat_count)
    fine_att = fine_window_attention(fine_query, fine_extended, row_valid, radius)
    queries = fine_query.reshape(-1, channels)
    lat_table = fold_poles(upsample_table(tile_rows), lat_index, lat_count)
    lon_table = upsample_table(tile_cols)
    cycle_keyval = coarse_extended[
        radius - 1 : radius + coarse_rows + 1, radius - 1 : radius + coarse_cols + 1
    ]
    up_keyval = (
        upsample(cycle_keyval, lat_table, lon_table).astype(jnp.bfloat16).reshape(-1, 2 * channels)
    )
    up_att = upsample(cycle_att, lat_table, lon_table).reshape(-1, channels)
    cross = attend(queries, up_keyval, None, HEADS)
    joined = (fine_att.astype(jnp.float32) + cross + up_att).astype(jnp.bfloat16)
    output = jnp.dot(joined, out_weight, preferred_element_type=jnp.float32).astype(jnp.bfloat16)
    return output.reshape(tile_rows, tile_cols, channels)


def solution(mesh):
    placed = (
        P("lat", "lon", None),
        P("lat", "lon", None),
        P("lat", "lon", None),
        P("lat", "lon", None),
        P(),
    )
    return jax.shard_map(
        shards, mesh=mesh, in_specs=placed, out_specs=P("lat", "lon", None), check_vma=False
    )
```

profile of v0, /device:TPU:0, one launch (start us, length us, event | category | flops | bytes accessed | tf_op | source)
XLA Modules:
  0.0 220.4 jit_solution(5592044522308787714)
XLA Ops:
  3.5 2.3 %copy.89 = bf16[24,32,1024]{2,0,1:T(8,128)(2,1)S(1)} copy(bf16[24,32,1024]{2,1,0:T(8,128)(2,1)} %param.22) | data formatting | bytes 3145728 | tf_op args[1]
  13.6 2.3 %collective-permute-start.6 = (bf16[18,6,1024]{2,0,1:T(8,128)(2,1)S(1)}, bf16[18,6,1024]{2,0,1:T(8,128)(2,1)S(1)}, u32[]{:S(2)}, u32[]{:S(2)}) collective-permute-start(bf16[18,6,1024]{2,0,1:T(8,128)(2,1)S(1)} %get-tuple-element.822), channel_id=1, source_target_pairs={{0,1},{1,2},{2,3},{3,4},{4,5},{5,6},{6,7},{7,0},{8,9},{9,10},{10,1... | collective-permute-start | bytes 663560 | tf_op jit(solution)/shard_map/ppermute | solution.py:21
  15.9 3.1 %collective-permute-start.7 = (bf16[18,6,1024]{2,0,1:T(8,128)(2,1)S(1)}, bf16[18,6,1024]{2,0,1:T(8,128)(2,1)S(1)}, u32[]{:S(2)}, u32[]{:S(2)}) collective-permute-start(bf16[18,6,1024]{2,0,1:T(8,128)(2,1)S(1)} %get-tuple-element.823), channel_id=1, source_target_pairs={{1,0},{2,1},{3,2},{4,3},{5,4},{6,5},{7,6},{0,7},{9,8},{10,9},{11,1... | collective-permute-start | bytes 663560 | tf_op jit(solution)/shard_map/ppermute | solution.py:24
  19.0 9.5 %collective-permute-done.6 = bf16[18,6,1024]{2,0,1:T(8,128)(2,1)S(1)} collective-permute-done((bf16[18,6,1024]{2,0,1:T(8,128)(2,1)S(1)}, bf16[18,6,1024]{2,0,1:T(8,128)(2,1)S(1)}, u32[]{:S(2)}, u32[]{:S(2)}) %collective-permute-start.6) | collective-permute-done | bytes 221216 | tf_op jit(solution)/shard_map/ppermute | solution.py:21
  28.5 2.2 collective-permute-done.7
  31.9 4.3 %convolution_convert_fusion = bf16[24,1024,32]{1,2,0:T(8,128)(2,1)} fusion(f32[24,10,1024]{2,0,1:T(8,128)S(1)} %fusion.49, f32[32]{0:T(128)S(1)} %get-tuple-element.836, s32[32]{0:T(128)S(1)} %get-tuple-element.839, f32[32]{0:T(128)S(1)} %abs_subtract_fusion, s32[32]{0:T(128)S(1)} %broadcast_add_fusion.1, f32[32]{0:T(128)S(1)} %get-tuple-element.837, ...), kind=kOutput, calls=%fused_computation.75 | convolution fusion | flops 95160832 | bytes 2556672 | tf_op jit(solution)/shard_map/jb,ibc->ijc/dot_general | solution.py:111
  36.3 2.6 %copy.98 = bf16[768,1024]{0,1:T(8,128)(2,1)} copy(bf16[768,1024]{1,0:T(8,128)(2,1)} %bitcast.136) | data formatting | bytes 3145728 | tf_op jit(solution)/shard_map/while | solution.py:83
  41.4 7.5 %while.76 = (s32[]{:T(128)}, bf16[48,512]{1,0:T(8,128)(2,1)S(1)}, bf16[360,1024]{0,1:T(8,128)(2,1)S(1)}, bf16[48,512]{1,0:T(8,128)(2,1)}, s32[48]{0:T(128)S(1)},...) while((s32[]{:T(128)}, bf16[48,512]{1,0:T(8,128)(2,1)S(1)}, ...), condition=%wide.region_16.17_spmd.clone, body=%wide.region_13.16_spmd.clone.sunk | while | flops 13721145 | bytes 1137838 | solution.py:83
  52.1 38.7 %while.75 = (s32[]{:T(128)}, f32[768,512]{1,0:T(8,128)}, bf16[768,1024]{0,1:T(8,128)(2,1)}, bf16[768,512]{1,0:T(8,128)(2,1)}, s32[]{:T(128)}, /*index=5*/s32[]{:T(128)}, s32[]{:T(128)}, s32[]{:T(128)}, s32[]{:T(128)}, s32[]{:T(128)}) while((s32[]{:T(128)}, f32[768,512]{1,0:T(8,128)}, bf16[768,1024]{0,1:T(8,128)(2,1)}, ...), condition=%wide.region_12.13_spmd, body=%wide.region_9.12_spmd.sunk | while | flops 307888896 | bytes 13578462 | solution.py:83
  54.3 3.7 %fusion.150 = (f32[2,768]{1,0:T(2,128)S(1)}, f32[2,768,768]{1,2,0:T(8,128)}) fusion(bf16[768,2,64]{0,2,1:T(8,128)(2,1)S(1)} %bitcast.137, bf16[768,2,64]{0,2,1:T(8,128)(2,1)S(1)} %bitcast.139), kind=kOutput, calls=%fused_computation.190.clone.1 | convolution fusion | flops 154534656 | bytes 5117952 | tf_op jit(solution)/shard_map/while/body/eval_jaxpr/sub | solution.py:73
  57.9 2.9 %fusion.151 = f32[2,64,768]{2,1,0:T(8,128)S(1)} fusion(bf16[768,2,64]{0,2,1:T(8,128)(2,1)S(1)} %bitcast.138, f32[2,768,768]{1,2,0:T(8,128)} %get-tuple-element.1033, f32[2,768]{1,0:T(2,128)S(1)} %get-tuple-element.1034), kind=kOutput, calls=%fused_computation.8.clone.1 | convolution fusion | flops 153354240 | bytes 5314560 | tf_op jit(solution)/shard_map/while/body/eval_jaxpr/gmn,ngd->mgd/dot_general | solution.py:76
  63.9 3.7 %fusion.150 = (f32[2,768]{1,0:T(2,128)S(1)}, f32[2,768,768]{1,2,0:T(8,128)}) fusion(bf16[768,2,64]{0,2,1:T(8,128)(2,1)S(1)} %bitcast.137, bf16[768,2,64]{0,2,1:T(8,128)(2,1)S(1)} %bitcast.139), kind=kOutput, calls=%fused_computation.190.clone.1 | convolution fusion | flops 154534656 | bytes 5117952 | tf_op jit(solution)/shard_map/while/body/eval_jaxpr/sub | solution.py:73
  67.6 2.9 %fusion.151 = f32[2,64,768]{2,1,0:T(8,128)S(1)} fusion(bf16[768,2,64]{0,2,1:T(8,128)(2,1)S(1)} %bitcast.138, f32[2,768,768]{1,2,0:T(8,128)} %get-tuple-element.1033, f32[2,768]{1,0:T(2,128)S(1)} %get-tuple-element.1034), kind=kOutput, calls=%fused_computation.8.clone.1 | convolution fusion | flops 153354240 | bytes 5314560 | tf_op jit(solution)/shard_map/while/body/eval_jaxpr/gmn,ngd->mgd/dot_general | solution.py:76
  73.6 3.7 %fusion.150 = (f32[2,768]{1,0:T(2,128)S(1)}, f32[2,768,768]{1,2,0:T(8,128)}) fusion(bf16[768,2,64]{0,2,1:T(8,128)(2,1)S(1)} %bitcast.137, bf16[768,2,64]{0,2,1:T(8,128)(2,1)S(1)} %bitcast.139), kind=kOutput, calls=%fused_computation.190.clone.1 | convolution fusion | flops 154534656 | bytes 5117952 | tf_op jit(solution)/shard_map/while/body/eval_jaxpr/sub | solution.py:73
  77.3 2.9 %fusion.151 = f32[2,64,768]{2,1,0:T(8,128)S(1)} fusion(bf16[768,2,64]{0,2,1:T(8,128)(2,1)S(1)} %bitcast.138, f32[2,768,768]{1,2,0:T(8,128)} %get-tuple-element.1033, f32[2,768]{1,0:T(2,128)S(1)} %get-tuple-element.1034), kind=kOutput, calls=%fused_computation.8.clone.1 | convolution fusion | flops 153354240 | bytes 5314560 | tf_op jit(solution)/shard_map/while/body/eval_jaxpr/gmn,ngd->mgd/dot_general | solution.py:76
  83.3 3.7 %fusion.150 = (f32[2,768]{1,0:T(2,128)S(1)}, f32[2,768,768]{1,2,0:T(8,128)}) fusion(bf16[768,2,64]{0,2,1:T(8,128)(2,1)S(1)} %bitcast.137, bf16[768,2,64]{0,2,1:T(8,128)(2,1)S(1)} %bitcast.139), kind=kOutput, calls=%fused_computation.190.clone.1 | convolution fusion | flops 154534656 | bytes 5117952 | tf_op jit(solution)/shard_map/while/body/eval_jaxpr/sub | solution.py:73
  86.9 2.9 %fusion.151 = f32[2,64,768]{2,1,0:T(8,128)S(1)} fusion(bf16[768,2,64]{0,2,1:T(8,128)(2,1)S(1)} %bitcast.138, f32[2,768,768]{1,2,0:T(8,128)} %get-tuple-element.1033, f32[2,768]{1,0:T(2,128)S(1)} %get-tuple-element.1034), kind=kOutput, calls=%fused_computation.8.clone.1 | convolution fusion | flops 153354240 | bytes 5314560 | tf_op jit(solution)/shard_map/while/body/eval_jaxpr/gmn,ngd->mgd/dot_general | solution.py:76
  91.2 4.4 %collective-permute-start.11 = (bf16[8,1,512]{2,0,1:T(8,128)(2,1)S(1)}, bf16[8,1,512]{2,0,1:T(8,128)(2,1)S(1)}, u32[]{:S(2)}, u32[]{:S(2)}) collective-permute-start(bf16[8,1,512]{2,0,1:T(8,128)(2,1)S(1)} %get-tuple-element.825), channel_id=1, source_target_pairs={{1,0},{2,1},{3,2},{4,3},{5,4},{6,5},{7,6},{0,7},{9,8},{10,9},{11,1... | collective-permute-start | bytes 24584 | tf_op jit(solution)/shard_map/ppermute | solution.py:24
  97.1 4.7 %collective-permute-start.3 = (bf16[36,6,1024]{2,0,1:T(8,128)(2,1)S(1)}, bf16[36,6,1024]{2,0,1:T(8,128)(2,1)S(1)}, u32[]{:S(2)}, u32[]{:S(2)}) collective-permute-start(bf16[36,6,1024]{2,0,1:T(8,128)(2,1)S(1)} %get-tuple-element.819), channel_id=1, source_target_pairs={{1,0},{2,1},{3,2},{4,3},{5,4},{6,5},{7,6},{0,7},{9,8},{10,9},{11,1... | collective-permute-start | bytes 1327112 | tf_op jit(solution)/shard_map/ppermute | solution.py:24
  102.2 2.9 %fusion.47 = f32[24,512,32]{1,2,0:T(8,128)} fusion(f32[24,10,512]{2,0,1:T(8,128)S(1)} %fusion.51, f32[32]{0:T(128)S(1)} %get-tuple-element.836, s32[32]{0:T(128)S(1)} %get-tuple-element.839, f32[32]{0:T(128)S(1)} %abs_subtract_fusion, s32[32]{0:T(128)S(1)} %broadcast_add_fusion.1, f32[32]{0:T(128)S(1)} %get-tuple-element.837, s32[32]{0:T(128)S(1)} %get-tuple-element.838), kind=kOutput, calls=%fused_computation.83 | convolution fusion | flops 47188480 | bytes 2065152 | tf_op jit(solution)/shard_map/jb,ibc->ijc/dot_general | solution.py:111
  105.1 11.8 %collective-permute-done.2 = bf16[36,6,1024]{2,0,1:T(8,128)(2,1)S(1)} collective-permute-done((bf16[36,6,1024]{2,0,1:T(8,128)(2,1)S(1)}, bf16[36,6,1024]{2,0,1:T(8,128)(2,1)S(1)}, u32[]{:S(2)}, u32[]{:S(2)}) %collective-permute-start.2) | collective-permute-done | bytes 442400 | tf_op jit(solution)/shard_map/ppermute | solution.py:21
  116.9 2.4 %collective-permute-done.3 = bf16[36,6,1024]{2,0,1:T(8,128)(2,1)S(1)} collective-permute-done((bf16[36,6,1024]{2,0,1:T(8,128)(2,1)S(1)}, bf16[36,6,1024]{2,0,1:T(8,128)(2,1)S(1)}, u32[]{:S(2)}, u32[]{:S(2)}) %collective-permute-start.3) | collective-permute-done | bytes 442400 | tf_op jit(solution)/shard_map/ppermute | solution.py:24
  119.4 2.5 %pad_maximum_fusion = bf16[36,44,1024]{2,0,1:T(8,128)(2,1)S(1)} fusion(bf16[36,6,1024]{2,0,1:T(8,128)(2,1)S(1)} %collective-permute-done.3, bf16[6,32,1024]{2,0,1:T(8,128)(2,1)} %collective-permute-done.1, bf16[24,32,1024]{2,0,1:T(8,128)(2,1)S(1)} %copy.89, bf16[6,32,1024]{2,0,1:T(8,128)(2,1)} %collective-permute-done, ...), kind=kLoop, calls=%fused_computation.74 | loop fusion | flops 16220160 | bytes 6488064 | tf_op jit(solution)/shard_map/concatenate | solution.py:25
  121.9 3.6 %copy.92 = bf16[36,44,1024]{2,1,0:T(8,128)(2,1)} copy(bf16[36,44,1024]{2,0,1:T(8,128)(2,1)S(1)} %pad_maximum_fusion) | data formatting | bytes 6488064 | tf_op jit(solution)/shard_map/while | solution.py:140
  125.5 89.7 %while.74 = (s32[]{:T(128)}, bf16[6,8,16,512]{3,2,1,0:T(8,128)(2,1)}, s32[6]{0:T(128)S(1)}, bf16[24,32,512]{2,1,0:T(8,128)(2,1)}, bf16[36,44,1024]{2,1,0:T(8,128...) while((s32[]{:T(128)}, ...), condition=%wide.region_5.6_spmd, body=%wide.region_0.5_spmd.sunk | while | flops 56924712 | bytes 10279354 | solution.py:140
  128.6 2.0 constant_dynamic-slice_fusion.19
  132.9 6.8 %while.77 = (s32[]{:T(128)}, bf16[128,512]{1,0:T(8,128)(2,1)S(1)}, bf16[560,1024]{0,1:T(8,128)(2,1)S(1)}, bf16[128,512]{1,0:T(8,128)(2,1)S(1)}, s32[128]{0:T(128...) while((s32[]{:T(128)}, bf16[128,512]{1,0:T(8,128)(2,1)S(1)}, ...), condition=%wide.region_4.4_spmd.clone, body=%wide.region_1.3_spmd.clone.sunk | while | flops 56915304 | bytes 2734262 | solution.py:83
  147.8 6.8 %while.77 = (s32[]{:T(128)}, bf16[128,512]{1,0:T(8,128)(2,1)S(1)}, bf16[560,1024]{0,1:T(8,128)(2,1)S(1)}, bf16[128,512]{1,0:T(8,128)(2,1)S(1)}, s32[128]{0:T(128...) while((s32[]{:T(128)}, bf16[128,512]{1,0:T(8,128)(2,1)S(1)}, ...), condition=%wide.region_4.4_spmd.clone, body=%wide.region_1.3_spmd.clone.sunk | while | flops 56915304 | bytes 2734262 | solution.py:83
  162.8 6.8 %while.77 = (s32[]{:T(128)}, bf16[128,512]{1,0:T(8,128)(2,1)S(1)}, bf16[560,1024]{0,1:T(8,128)(2,1)S(1)}, bf16[128,512]{1,0:T(8,128)(2,1)S(1)}, s32[128]{0:T(128...) while((s32[]{:T(128)}, bf16[128,512]{1,0:T(8,128)(2,1)S(1)}, ...), condition=%wide.region_4.4_spmd.clone, body=%wide.region_1.3_spmd.clone.sunk | while | flops 56915304 | bytes 2734262 | solution.py:83
  177.7 6.8 %while.77 = (s32[]{:T(128)}, bf16[128,512]{1,0:T(8,128)(2,1)S(1)}, bf16[560,1024]{0,1:T(8,128)(2,1)S(1)}, bf16[128,512]{1,0:T(8,128)(2,1)S(1)}, s32[128]{0:T(128...) while((s32[]{:T(128)}, bf16[128,512]{1,0:T(8,128)(2,1)S(1)}, ...), condition=%wide.region_4.4_spmd.clone, body=%wide.region_1.3_spmd.clone.sunk | while | flops 56915304 | bytes 2734262 | solution.py:83
  192.7 6.8 %while.77 = (s32[]{:T(128)}, bf16[128,512]{1,0:T(8,128)(2,1)S(1)}, bf16[560,1024]{0,1:T(8,128)(2,1)S(1)}, bf16[128,512]{1,0:T(8,128)(2,1)S(1)}, s32[128]{0:T(128...) while((s32[]{:T(128)}, bf16[128,512]{1,0:T(8,128)(2,1)S(1)}, ...), condition=%wide.region_4.4_spmd.clone, body=%wide.region_1.3_spmd.clone.sunk | while | flops 56915304 | bytes 2734262 | solution.py:83
  207.6 6.8 %while.77 = (s32[]{:T(128)}, bf16[128,512]{1,0:T(8,128)(2,1)S(1)}, bf16[560,1024]{0,1:T(8,128)(2,1)S(1)}, bf16[128,512]{1,0:T(8,128)(2,1)S(1)}, s32[128]{0:T(128...) while((s32[]{:T(128)}, bf16[128,512]{1,0:T(8,128)(2,1)S(1)}, ...), condition=%wide.region_4.4_spmd.clone, body=%wide.region_1.3_spmd.clone.sunk | while | flops 56915304 | bytes 2734262 | solution.py:83
  (421 shorter events, 114.9 us)
Async XLA Ops:
  0.0 219.0 %copy-start = (bf16[512,512]{1,0:T(8,128)(2,1)S(1)}, bf16[512,512]{1,0:T(8,128)(2,1)}, u32[]{:S(2)}) copy-start(bf16[512,512]{1,0:T(8,128)(2,1)} %param.25) | copy-start | bytes 1572868
  1.0 12.3 %collective-permute-start.4 = (bf16[6,8,1024]{2,0,1:T(8,128)(2,1)S(1)}, bf16[6,8,1024]{2,0,1:T(8,128)(2,1)S(1)}, u32[]{:S(2)}, u32[]{:S(2)}) collective-permute-start(bf16[6,8,1024]{2,0,1:T(8,128)(2,1)S(1)} %copy.94), channel_id=1, source_target_pairs={{0,8},{8,16},{16,24},{24,0},{1,9},{9,17},{17,25},{25,1},{2,10},{10... | collective-permute-start | bytes 294920 | tf_op jit(solution)/shard_map/ppermute | solution.py:21
  1.5 11.8 %collective-permute-start.5 = (bf16[6,8,1024]{2,0,1:T(8,128)(2,1)S(1)}, bf16[6,8,1024]{2,0,1:T(8,128)(2,1)S(1)}, u32[]{:S(2)}, u32[]{:S(2)}) collective-permute-start(bf16[6,8,1024]{2,0,1:T(8,128)(2,1)S(1)} %copy.94), channel_id=1, source_target_pairs={{8,0},{16,8},{24,16},{0,24},{9,1},{17,9},{25,17},{1,25},{10,2},{18... | collective-permute-start | bytes 294920 | tf_op jit(solution)/shard_map/ppermute | solution.py:24
  7.0 88.6 %collective-permute-start = (bf16[6,32,1024]{2,0,1:T(8,128)(2,1)}, bf16[6,32,1024]{2,0,1:T(8,128)(2,1)}, u32[]{:S(2)}, u32[]{:S(2)}) collective-permute-start(bf16[6,32,1024]{2,0,1:T(8,128)(2,1)} %get-tuple-element.820), channel_id=1, source_target_pairs={{0,8},{8,16},{16,24},{24,0},{1,9},{9,17},{17,25},{25,1},{2,10},{10... | collective-permute-start | bytes 1179656 | tf_op jit(solution)/shard_map/ppermute | solution.py:21
  7.6 88.0 %collective-permute-start.1 = (bf16[6,32,1024]{2,0,1:T(8,128)(2,1)}, bf16[6,32,1024]{2,0,1:T(8,128)(2,1)}, u32[]{:S(2)}, u32[]{:S(2)}) collective-permute-start(bf16[6,32,1024]{2,0,1:T(8,128)(2,1)} %get-tuple-element.821), channel_id=1, source_target_pairs={{8,0},{16,8},{24,16},{0,24},{9,1},{17,9},{25,17},{1,25},{10,2},{18... | collective-permute-start | bytes 1179656 | tf_op jit(solution)/shard_map/ppermute | solution.py:24
  13.6 14.9 %collective-permute-start.6 = (bf16[18,6,1024]{2,0,1:T(8,128)(2,1)S(1)}, bf16[18,6,1024]{2,0,1:T(8,128)(2,1)S(1)}, u32[]{:S(2)}, u32[]{:S(2)}) collective-permute-start(bf16[18,6,1024]{2,0,1:T(8,128)(2,1)S(1)} %get-tuple-element.822), channel_id=1, source_target_pairs={{0,1},{1,2},{2,3},{3,4},{4,5},{5,6},{6,7},{7,0},{8,9},{9,10},{10,1... | collective-permute-start | bytes 663560 | tf_op jit(solution)/shard_map/ppermute | solution.py:21
  15.9 14.8 %collective-permute-start.7 = (bf16[18,6,1024]{2,0,1:T(8,128)(2,1)S(1)}, bf16[18,6,1024]{2,0,1:T(8,128)(2,1)S(1)}, u32[]{:S(2)}, u32[]{:S(2)}) collective-permute-start(bf16[18,6,1024]{2,0,1:T(8,128)(2,1)S(1)} %get-tuple-element.823), channel_id=1, source_target_pairs={{1,0},{2,1},{3,2},{4,3},{5,4},{6,5},{7,6},{0,7},{9,8},{10,9},{11,1... | collective-permute-start | bytes 663560 | tf_op jit(solution)/shard_map/ppermute | solution.py:24
  48.9 41.9 %collective-permute-start.8 = (bf16[1,8,512]{2,0,1:T(2,128)(2,1)S(1)}, bf16[1,8,512]{2,0,1:T(2,128)(2,1)S(1)}, u32[]{:S(2)}, u32[]{:S(2)}) collective-permute-start(bf16[1,8,512]{2,0,1:T(2,128)(2,1)S(1)} %copy.103), channel_id=1, source_target_pairs={{0,8},{8,16},{16,24},{24,0},{1,9},{9,17},{17,25},{25,1},{2,10},{10... | collective-permute-start | bytes 24584 | tf_op jit(solution)/shard_map/ppermute | solution.py:21
  49.0 41.8 %collective-permute-start.9 = (bf16[1,8,512]{2,0,1:T(2,128)(2,1)S(1)}, bf16[1,8,512]{2,0,1:T(2,128)(2,1)S(1)}, u32[]{:S(2)}, u32[]{:S(2)}) collective-permute-start(bf16[1,8,512]{2,0,1:T(2,128)(2,1)S(1)} %copy.104), channel_id=1, source_target_pairs={{8,0},{16,8},{24,16},{0,24},{9,1},{17,9},{25,17},{1,25},{10,2},{18... | collective-permute-start | bytes 24584 | tf_op jit(solution)/shard_map/ppermute | solution.py:24
  90.9 11.0 %collective-permute-start.10 = (bf16[8,1,512]{2,0,1:T(8,128)(2,1)S(1)}, bf16[8,1,512]{2,0,1:T(8,128)(2,1)S(1)}, u32[]{:S(2)}, u32[]{:S(2)}) collective-permute-start(bf16[8,1,512]{2,0,1:T(8,128)(2,1)S(1)} %get-tuple-element.824), channel_id=1, source_target_pairs={{0,1},{1,2},{2,3},{3,4},{4,5},{5,6},{6,7},{7,0},{8,9},{9,10},{10,1... | collective-permute-start | bytes 24584 | tf_op jit(solution)/shard_map/ppermute | solution.py:21
  91.2 10.6 %collective-permute-start.11 = (bf16[8,1,512]{2,0,1:T(8,128)(2,1)S(1)}, bf16[8,1,512]{2,0,1:T(8,128)(2,1)S(1)}, u32[]{:S(2)}, u32[]{:S(2)}) collective-permute-start(bf16[8,1,512]{2,0,1:T(8,128)(2,1)S(1)} %get-tuple-element.825), channel_id=1, source_target_pairs={{1,0},{2,1},{3,2},{4,3},{5,4},{6,5},{7,6},{0,7},{9,8},{10,9},{11,1... | collective-permute-start | bytes 24584 | tf_op jit(solution)/shard_map/ppermute | solution.py:24
  97.0 19.9 %collective-permute-start.2 = (bf16[36,6,1024]{2,0,1:T(8,128)(2,1)S(1)}, bf16[36,6,1024]{2,0,1:T(8,128)(2,1)S(1)}, u32[]{:S(2)}, u32[]{:S(2)}) collective-permute-start(bf16[36,6,1024]{2,0,1:T(8,128)(2,1)S(1)} %get-tuple-element.818), channel_id=1, source_target_pairs={{0,1},{1,2},{2,3},{3,4},{4,5},{5,6},{6,7},{7,0},{8,9},{9,10},{10,1... | collective-permute-start | bytes 1327112 | tf_op jit(solution)/shard_map/ppermute | solution.py:21
  97.1 22.3 %collective-permute-start.3 = (bf16[36,6,1024]{2,0,1:T(8,128)(2,1)S(1)}, bf16[36,6,1024]{2,0,1:T(8,128)(2,1)S(1)}, u32[]{:S(2)}, u32[]{:S(2)}) collective-permute-start(bf16[36,6,1024]{2,0,1:T(8,128)(2,1)S(1)} %get-tuple-element.819), channel_id=1, source_target_pairs={{1,0},{2,1},{3,2},{4,3},{5,4},{6,5},{7,6},{0,7},{9,8},{10,9},{11,1... | collective-permute-start | bytes 1327112 | tf_op jit(solution)/shard_map/ppermute | solution.py:24
  216.5 1.4 copy-start.1
  216.5 1.9 copy-start.2
where the time goes:
time: 222 us; the launch traced here: 220 us
  local copies, waits for them, and re-layouts  73.1 us (33%)
  matrix products  63.6 us (29%)
  waiting for transfers between devices  25.9 us (12%)
  starting transfers between devices  21 us (9%)
  loops' own time  18.4 us (8%)
  other arithmetic  18.1 us (8%)
    sub x32, matrix products, one_group(): logit_scores = logit_scores - jnp.max(logit_scores, axis=-1, keepdims=True)  26.1 us
    ppermute x6, waiting for transfers between devices, with_halo(): lax.ppermute(lax.slice_in_dim(block, block.shape[dim] - width, None, axis...  21.3 us
    dot_general x32, matrix products, one_group(): jnp.einsum('gmn,ngd->mgd', softmax_weights, value_portion, preferred_elem...  20.3 us
    ppermute x6, starting transfers between devices, with_halo(): lax.ppermute(lax.slice_in_dim(block, 0, width, axis=dim), axis, backward)  17.1 us
    another operation x1, loops' own time, fine_window_attention(): blocks = lax.map(one_block, jnp.arange(down * across, dtype=jnp.int32))  15.9 us
    dynamic_slice x6, local copies, waits for them, and re-layouts, one_block(): lax.dynamic_slice(fine_extended, (row_start, col_start, zero), (block_row...  11.9 us
    dynamic_slice x60, local copies, waits for them, and re-layouts, one_group(): lax.dynamic_slice_in_dim(queries, block * group_span, group_span, 1)  10.2 us
    and x28, other arithmetic, window_allowed(): (jnp.abs(lat_gap) <= radius) & (jnp.abs(lon_gap) <= radius)  7.59 us
  transfers between devices with their start and end apart: 12, of which 4 were waited for; matrix products, arithmetic and copies ran while one was open for 32% of the time, Pallas kernels for 0%

commit v1 on v0

v1 whole, which is shorter than its diff:
```python
import math

import jax
import jax.numpy as jnp
import numpy as np
from jax import lax
from jax.experimental import pallas as pl
from jax.experimental.pallas import tpu as pltpu
from jax.sharding import PartitionSpec as P

HEADS = 8
RADIUS = 6
FACTOR = 4
ROWS, COLS = 24, 32
CROWS, CCOLS = 6, 8
LANES = 128
BLOCK_ROWS = 8
BLOCKS = ROWS // BLOCK_ROWS
BLOCK = BLOCK_ROWS * COLS
MASKED = -16384.0
EXPONENT = 0.125 * math.log2(math.e)
F32 = jnp.float32
BF16 = jnp.bfloat16


ROW_ORDER = list(range(2, 22)) + [0, 1, 22, 23]
LEFT_FINE = [(r, c - RADIUS) for r in ROW_ORDER for c in range(RADIUS)]
RIGHT_FINE = [(r, COLS + c) for r in ROW_ORDER for c in range(RADIUS)]
CORNER_TOP = list(range(0, 24)) + list(range(120, 132))
CORNER_BOTTOM = list(range(96, 120)) + list(range(132, 144))
CORNERS = 36
LATE_ROWS = 96


def own_range(block):
    first = max(0, block * BLOCK_ROWS - RADIUS)
    last = min(ROWS, (block + 1) * BLOCK_ROWS + RADIUS)
    return first * COLS, last * COLS


def lon_slices(block):
    return (((0, 80), (112, 144)), ((0, 128),), ((32, 144),))[block]


def corner_keys(top):
    picks = CORNER_BOTTOM if top else CORNER_TOP
    shift = -ROWS if top else ROWS
    keys = [(LEFT_FINE[i][0] + shift, LEFT_FINE[i][1]) for i in picks]
    keys += [(RIGHT_FINE[i][0] + shift, RIGHT_FINE[i][1]) for i in picks]
    return keys + [None] * (LATE_ROWS - len(keys))


def side_keys(block):
    keys = []
    if block == 0:
        keys += [(r - RADIUS, c) for r in range(RADIUS) for c in range(COLS)]
    if block == BLOCKS - 1:
        keys += [(r + ROWS, c) for r in range(RADIUS) for c in range(COLS)]
    for side in (LEFT_FINE, RIGHT_FINE):
        for low, high in lon_slices(block):
            keys += side[low:high]
    return keys


def mask_lanes(keys, rows, cols):
    table = np.zeros((len(keys), LANES), np.float32)
    for n, key in enumerate(keys):
        if key is None:
            table[n, : len(rows) + len(cols)] = MASKED
            continue
        for i, row in enumerate(rows):
            if abs(key[0] - row) > RADIUS:
                table[n, i] = MASKED
        for j, col in enumerate(cols):
            if abs(key[1] - col) > RADIUS:
                table[n, len(rows) + j] = MASKED
    return table


def chosen_lanes(queries, rows, cols):
    table = np.zeros((len(queries), LANES), np.float32)
    for n, query in enumerate(queries):
        if query is None:
            continue
        table[n, rows.index(query[0])] = 1.0
        table[n, len(rows) + cols.index(query[1])] = 1.0
        table[n, LANES - 1] = 1.0
    return table


def block_rows(block):
    return list(range(block * BLOCK_ROWS, (block + 1) * BLOCK_ROWS))


FINE_COLS = list(range(COLS))
FINE_CHOSEN = chosen_lanes(
    [(r, c) for r in range(BLOCK_ROWS) for c in range(COLS)], list(range(BLOCK_ROWS)), FINE_COLS
)
OWN_MASK = np.concatenate(
    [
        mask_lanes(
            [(n // COLS, n % COLS) for n in range(*own_range(b))], block_rows(b), FINE_COLS
        )
        for b in range(BLOCKS)
    ]
)
SIDE_MASK = np.concatenate(
    [mask_lanes(side_keys(b), block_rows(b), FINE_COLS) for b in range(BLOCKS)]
)
SIDE_SIZES = [len(side_keys(b)) for b in range(BLOCKS)]
EDGE = RADIUS * COLS
CORNER_MASK = np.concatenate(
    [
        mask_lanes(corner_keys(True), block_rows(0), FINE_COLS),
        mask_lanes(corner_keys(False), block_rows(BLOCKS - 1), FINE_COLS),
    ]
)

CQ_COLS = list(range(-1, CCOLS + 1))
OWN_COARSE = [(r, c) for r in range(CROWS) for c in range(CCOLS)]
LEFT_COARSE = [(r, c - 7) for r in range(CROWS) for c in range(7)] + [None] * CROWS
RIGHT_COARSE = [(r, c + CCOLS) for r in range(CROWS) for c in range(7)] + [None] * CROWS
BAND = OWN_COARSE + LEFT_COARSE + RIGHT_COARSE


def moved(keys, rows):
    return [None if key is None else (key[0] + rows, key[1]) for key in keys]


COARSE_KEYS = BAND + moved(BAND, -CROWS) + moved(BAND, CROWS)
COARSE_COUNT = 512
COARSE_KEYS = COARSE_KEYS + [None] * (COARSE_COUNT - len(COARSE_KEYS))
COARSE_QUERIES = (
    OWN_COARSE
    + [None] * 10
    + [(r, -1) for r in range(CROWS)]
    + [None] * 10
    + [(r, CCOLS) for r in range(CROWS)]
)
COARSE_CHOSEN = chosen_lanes(COARSE_QUERIES, list(range(CROWS)), CQ_COLS)
COARSE_MASK = mask_lanes(COARSE_KEYS, list(range(CROWS)), CQ_COLS)
LATE_ATT = (
    [None] * 8
    + [(0, c) for c in range(CCOLS)]
    + [(0, -1), (0, CCOLS)]
    + [None] * (LATE_ROWS - 2 * CORNERS - 10)
)
ATT_CELLS = COARSE_QUERIES + moved(LATE_ATT, -1) + moved(LATE_ATT, CROWS)


def coefficient(fine):
    coarse, offset = fine // FACTOR, (fine % FACTOR - 1.5) / FACTOR
    taps = {coarse: 1.0 - abs(offset)}
    taps[coarse + (1 if offset > 0 else -1)] = abs(offset)
    return taps


def up_table(fine_cells, coarse_cells, pole):
    where = {cell: n for n, cell in reversed(list(enumerate(coarse_cells))) if cell is not None}
    table = np.zeros((len(fine_cells), len(coarse_cells)), np.float32)
    for n, (row, col) in enumerate(fine_cells):
        for r, a in coefficient(row).items():
            if pole == "top":
                r = max(r, 0)
            if pole == "bottom":
                r = min(r, CROWS - 1)
            for c, b in coefficient(col).items():
                table[n, where[(r, c)]] += a * b
    return table


def poles(fine_cells, coarse_cells):
    return np.stack([up_table(fine_cells, coarse_cells, p) for p in ("none", "top", "bottom")])


FINE_CELLS = [(r, c) for r in range(ROWS) for c in range(COLS)]
INNER = [(r, c) for r in range(2, ROWS - 2) for c in range(2, COLS - 2)]
EARLY_COUNT = 512
EARLY_CELLS = INNER[:EARLY_COUNT]
LATE_CELLS = [cell for cell in FINE_CELLS if cell not in set(EARLY_CELLS)]
UP_EARLY = up_table(EARLY_CELLS, OWN_COARSE, "none")
UP_LATE = poles(LATE_CELLS, COARSE_KEYS)
UP_ATT = poles(FINE_CELLS, ATT_CELLS)


def picked(indices, count):
    table = np.zeros((len(indices), count), np.float32)
    for n, index in enumerate(indices):
        if index is not None:
            table[n, index] = 1.0
    return table


FINE_EAST = [r * COLS + COLS - RADIUS + c for r in ROW_ORDER for c in range(RADIUS)]
FINE_WEST = [r * COLS + c for r in ROW_ORDER for c in range(RADIUS)]
PICK_FINE = picked(FINE_EAST + FINE_WEST, ROWS * COLS)
PICK_COARSE = picked(
    [r * CCOLS + 1 + c for r in range(CROWS) for c in range(7)]
    + [None] * CROWS
    + [r * CCOLS + c for r in range(CROWS) for c in range(7)]
    + [None] * CROWS,
    CROWS * CCOLS,
)
PICK_QUERY = picked(
    [None] * 42
    + [r * CCOLS + CCOLS - 1 for r in range(CROWS)]
    + [None] * 42
    + [r * CCOLS for r in range(CROWS)],
    CROWS * CCOLS,
)
SIDE = len(ROW_ORDER) * RADIUS


def late_picks(corner, row):
    rest = LATE_ROWS - 2 * CORNERS
    left = picked(list(corner) + [None] * (CORNERS + rest), SIDE)
    right = picked([None] * CORNERS + list(corner) + [None] * rest, SIDE)
    cells = [(row, c) for c in range(CCOLS)] + [(row, -1), (row, CCOLS)]
    att = [None] * (2 * CORNERS) + [COARSE_QUERIES.index(cell) for cell in cells]
    att = picked(att + [None] * (LATE_ROWS - len(att)), len(COARSE_QUERIES))
    return left, right, att


LATE_PICKS = [
    np.concatenate(tables)
    for tables in zip(late_picks(CORNER_BOTTOM, CROWS - 1), late_picks(CORNER_TOP, 0))
]


PAIRS = HEADS // 2
LEAST, MOST = 2.0**-80, 2.0**100


def halves():
    return lax.broadcasted_iota(jnp.int32, (1, LANES), 1) < LANES // 2


def head_of(pair, head):
    return jnp.where(halves() == (head == 0), pair, jnp.zeros((), pair.dtype))


def packed(first, second):
    return jnp.where(halves(), first, second)


def dot(a, b):
    return jnp.dot(a, b, preferred_element_type=F32)


def scores(queries, keys):
    return lax.dot_general(queries, keys, (((1,), (1,)), ((), ())), preferred_element_type=F32)


def mix(weights, values):
    mixed = dot(weights.astype(BF16), values)
    return mixed[:, :LANES], mixed[:, LANES:]


def with_ones(values):
    return jnp.concatenate([values, jnp.ones_like(values)], 1)


def pole_flags():
    lat = lax.axis_index("lat")
    return lat == 0, lat == lax.axis_size("lat") - 1


def low(pair):
    return pl.ds(pl.multiple_of(pair * LANES, LANES), LANES)


def high(pair):
    return pl.ds(pl.multiple_of((pair + PAIRS) * LANES, LANES), LANES)


def close_edge(mask, closed):
    lane = lax.broadcasted_iota(jnp.int32, (1, LANES), 1)
    return jnp.where((lane == LANES - 1) & closed, MASKED, mask.astype(F32)).astype(BF16)


def plain_softmax(queries, chosen, keys, values):
    mixed, total = [], []
    for head in range(2):
        query = head_of(queries, head)
        if chosen is not None:
            query = jnp.concatenate([query, chosen], 1)
        a, b = mix(jnp.exp2(scores(query, keys) * EXPONENT), values)
        mixed.append(a)
        total.append(b)
    return packed(*mixed), packed(*total)


def exact_softmax(queries, chosen, keys, values):
    results = []
    for head in range(2):
        query = head_of(queries, head)
        if chosen is not None:
            query = jnp.concatenate([query, chosen], 1)
        score = scores(query, keys)
        score = score - jnp.max(score, 1, keepdims=True)
        mixed, total = mix(jnp.exp2(score * EXPONENT), values)
        results.append(mixed / total)
    return packed(*results)


def send_east_west_kernel(fkv_ref, ckv_ref, cq_ref, pf_ref, pc_ref, pq_ref, ce_ref, cw_ref, fe_ref, fw_ref):
    channels = cq_ref.shape[1]
    coarse = dot(pc_ref[...], ckv_ref[...])
    query = dot(pq_ref[...], cq_ref[...])
    coarse = jnp.concatenate([coarse[:, :channels] + query, coarse[:, channels:]], 1).astype(BF16)
    ce_ref[...], cw_ref[...] = coarse[:48], coarse[48:]
    fine = dot(pf_ref[...], fkv_ref[...]).astype(BF16)
    fe_ref[...], fw_ref[...] = fine[:SIDE], fine[SIDE:]


def send_band_kernel(fkv_ref, ckv_ref, left_ref, right_ref, south_ref, north_ref):
    for ref, first in ((south_ref, fkv_ref.shape[0] - EDGE), (north_ref, 0)):
        ref[0:EDGE, :] = fkv_ref[first : first + EDGE, :]
        ref[EDGE : EDGE + 48, :] = ckv_ref[...]
        ref[EDGE + 48 : EDGE + 96, :] = left_ref[...]
        ref[EDGE + 96 : EDGE + 144, :] = right_ref[...]


def send_late_kernel(left_ref, right_ref, att_ref, pl_ref, pr_ref, pa_ref, south_ref, north_ref):
    channels = att_ref.shape[1]
    sides = dot(pl_ref[...], left_ref[...]) + dot(pr_ref[...], right_ref[...])
    att = dot(pa_ref[...], att_ref[...])
    late = jnp.concatenate([sides[:, :channels] + att, sides[:, channels:]], 1).astype(BF16)
    south_ref[...], north_ref[...] = late[:LATE_ROWS], late[LATE_ROWS:]


def early_kernel(q_ref, kv_ref, ckv_ref, up_ref, chosen_ref, mask_ref, of_ref, lf_ref, oc_ref, lc_ref):
    up = up_ref[...]
    chosen = chosen_ref[...]

    @pl.loop(0, PAIRS)
    def _(pair):
        lo, hi = low(pair), high(pair)
        up_keys = dot(up, ckv_ref[:, lo]).astype(BF16)
        up_values = with_ones(dot(up, ckv_ref[:, hi]).astype(BF16))
        offset = 0
        for block in range(BLOCKS):
            first, last = own_range(block)
            mask = mask_ref[offset : offset + last - first, :]
            offset += last - first
            keys = jnp.concatenate([kv_ref[first:last, lo], mask], 1)
            values = with_ones(kv_ref[first:last, hi])
            rows = slice(block * BLOCK, (block + 1) * BLOCK)
            queries = q_ref[rows, lo]
            of_ref[rows, lo], lf_ref[rows, lo] = plain_softmax(queries, chosen, keys, values)
            oc_ref[rows, lo], lc_ref[rows, lo] = plain_softmax(queries, None, up_keys, up_values)


def gathered(refs, lanes):
    own, left, right, top, bottom = refs
    pad = jnp.zeros((COARSE_COUNT - 3 * len(BAND), LANES), BF16)
    return jnp.concatenate(
        [own[:, lanes], left[:, lanes], right[:, lanes], top[EDGE:, lanes], bottom[EDGE:, lanes], pad], 0
    )


def coarse_kernel(q_ref, own_ref, left_ref, right_ref, top_ref, bottom_ref, chosen_ref, mask_ref, out_ref):
    parts = (own_ref, left_ref, right_ref, top_ref, bottom_ref)
    is_top, is_bottom = pole_flags()
    band = len(BAND)
    mask = [
        mask_ref[:band, :],
        close_edge(mask_ref[band : 2 * band, :], is_top),
        close_edge(mask_ref[2 * band :, :], is_bottom),
    ]
    mask = jnp.concatenate(mask, 0)
    chosen = chosen_ref[...]

    @pl.loop(0, PAIRS)
    def _(pair):
        lo, hi = low(pair), high(pair)
        keys = jnp.concatenate([gathered(parts, lo), mask], 1)
        values = with_ones(gathered(parts, hi))
        queries = jnp.concatenate([q_ref[:, lo], left_ref[32:48, lo], right_ref[32:48, lo]], 0)
        out_ref[:, lo] = exact_softmax(queries, chosen, keys, values).astype(BF16)


def side_parts(block, left, right, top, bottom, lanes):
    parts = []
    if block == 0:
        parts.append(top[0:EDGE, lanes])
    if block == BLOCKS - 1:
        parts.append(bottom[0:EDGE, lanes])
    for side in (left, right):
        for a, b in lon_slices(block):
            parts.append(side[a:b, lanes])
    return jnp.concatenate(parts, 0)


def side_masks(mask_ref):
    is_top, is_bottom = pole_flags()
    masks, offset = [], 0
    for block in range(BLOCKS):
        mask = mask_ref[offset : offset + SIDE_SIZES[block], :]
        offset += SIDE_SIZES[block]
        if block in (0, BLOCKS - 1):
            edge = close_edge(mask[:EDGE], is_top if block == 0 else is_bottom)
            mask = jnp.concatenate([edge, mask[EDGE:]], 0)
        masks.append(mask)
    return masks


def late_up(parts, table, pair):
    up_keys = dot(table, gathered(parts, low(pair))).astype(BF16)
    return up_keys, dot(table, gathered(parts, high(pair))).astype(BF16)


def pole_table():
    is_top, is_bottom = pole_flags()
    return jnp.where(is_top, 1, jnp.where(is_bottom, 2, 0))


def middle_kernel(
    q_ref, of_ref, lf_ref, oc_ref, lc_ref, left_ref, right_ref, top_ref, bottom_ref,
    ckv_ref, cl_ref, cr_ref, chosen_ref, mask_ref, late_ref, fo_ref, fl_ref, cross_ref,
):
    parts = (ckv_ref, cl_ref, cr_ref, top_ref, bottom_ref)
    late = late_ref[pole_table()]
    chosen = chosen_ref[...]
    masks = side_masks(mask_ref)

    @pl.loop(0, PAIRS)
    def _(pair):
        lo, hi = low(pair), high(pair)
        up_keys, up_values = late_up(parts, late, pair)
        up_values = with_ones(up_values)
        for block in range(BLOCKS):
            sides = (left_ref, right_ref, top_ref, bottom_ref)
            keys = jnp.concatenate([side_parts(block, *sides, lo), masks[block]], 1)
            values = with_ones(side_parts(block, *sides, hi))
            rows = slice(block * BLOCK, (block + 1) * BLOCK)
            queries = q_ref[rows, lo]
            mixed, total = plain_softmax(queries, chosen, keys, values)
            fo_ref[rows, lo] = of_ref[rows, lo] + mixed
            fl_ref[rows, lo] = lf_ref[rows, lo] + total
            mixed, total = plain_softmax(queries, None, up_keys, up_values)
            cross_ref[rows, lo] = settled(oc_ref[rows, lo] + mixed, lc_ref[rows, lo] + total)


def settled(mixed, total):
    fits = (total > LEAST) & (total < MOST)
    return jnp.where(fits, mixed / total, jnp.nan)


def late_kernel(
    q_ref, fo_ref, fl_ref, cross_ref, lt_ref, lb_ref, att_ref, chosen_ref, mask_ref, up_ref, weight_ref,
    kv_hbm, left_ref, right_ref, top_ref, bottom_ref, ckv_ref, cl_ref, cr_ref,
    own_mask_hbm, side_mask_hbm, early_hbm, late_hbm,
    out_ref, joined_ref, bad_ref, kv_ref, own_mask_ref, side_mask_ref, early_ref, late_ref, sems,
):
    cells = q_ref.shape[0]
    is_top, is_bottom = pole_flags()
    pole = pole_table()
    corner_masks = [
        close_edge(mask_ref[:LATE_ROWS, :], is_top), close_edge(mask_ref[LATE_ROWS:, :], is_bottom)
    ]
    corner_rows = (slice(0, EDGE), slice(cells - EDGE, cells))
    corner_chosen = (slice(0, EDGE), slice(BLOCK - EDGE, BLOCK))
    up = up_ref[pole]
    bad_ref[...] = jnp.zeros_like(bad_ref)

    def up_att(pair):
        lo = low(pair)
        return dot(up, jnp.concatenate([att_ref[:, lo], lt_ref[64:96, lo], lb_ref[64:96, lo]], 0))

    @pl.loop(0, PAIRS)
    def _(pair):
        lo, hi = low(pair), high(pair)
        raised = up_att(pair)
        pieces = []
        for rows, picks, mask, late in zip(corner_rows, corner_chosen, corner_masks, (lt_ref, lb_ref)):
            keys = jnp.concatenate([late[:, lo], mask], 1)
            values = with_ones(late[:, hi])
            mixed, total = plain_softmax(q_ref[rows, lo], chosen_ref[picks, :], keys, values)
            pieces.append((rows, fo_ref[rows, lo] + mixed, fl_ref[rows, lo] + total))
        rows = slice(EDGE, cells - EDGE)
        pieces.append((rows, fo_ref[rows, lo], fl_ref[rows, lo]))
        for rows, mixed, total in pieces:
            fine = settled(mixed, total).astype(BF16).astype(F32)
            joined = fine + cross_ref[rows, lo] + raised[rows, :]
            joined_ref[pair, rows, :] = joined.astype(BF16)
            bad_ref[...] += jnp.sum(joined.reshape(-1, 8, LANES) * 0.0, 0)

    @pl.when(jnp.logical_not(jnp.sum(bad_ref[...]) == 0.0))
    def _():
        moves = [(kv_hbm, kv_ref), (own_mask_hbm, own_mask_ref), (side_mask_hbm, side_mask_ref),
                 (early_hbm, early_ref), (late_hbm, late_ref)]
        copies = [pltpu.make_async_copy(a, b, sems.at[n]) for n, (a, b) in enumerate(moves)]
        for copy in copies:
            copy.start()
        for copy in copies:
            copy.wait()
        parts = (ckv_ref, cl_ref, cr_ref, top_ref, bottom_ref)
        sides = (left_ref, right_ref, top_ref, bottom_ref)
        masks = side_masks(side_mask_ref)
        chosen = chosen_ref[...]

        @pl.loop(0, PAIRS)
        def _(pair):
            lo, hi = low(pair), high(pair)
            up_keys, up_values = late_up(parts, late_ref[pole], pair)
            up_keys = jnp.concatenate([dot(early_ref[...], ckv_ref[:, lo]).astype(BF16), up_keys], 0)
            up_values = jnp.concatenate([dot(early_ref[...], ckv_ref[:, hi]).astype(BF16), up_values], 0)
            up_values = with_ones(up_values)
            raised = up_att(pair)
            offset = 0
            for block in range(BLOCKS):
                first, last = own_range(block)
                mask = [own_mask_ref[offset : offset + last - first, :], masks[block]]
                offset += last - first
                keys = [kv_ref[first:last, lo], side_parts(block, *sides, lo)]
                values = [kv_ref[first:last, hi], side_parts(block, *sides, hi)]
                if block in (0, BLOCKS - 1):
                    late = lt_ref if block == 0 else lb_ref
                    mask.append(corner_masks[0 if block == 0 else 1])
                    keys.append(late[:, lo])
                    values.append(late[:, hi])
                keys = jnp.concatenate([jnp.concatenate(keys, 0), jnp.concatenate(mask, 0)], 1)
                values = with_ones(jnp.concatenate(values, 0))
                rows = slice(block * BLOCK, (block + 1) * BLOCK)
                queries = q_ref[rows, lo]
                fine = exact_softmax(queries, chosen, keys, values).astype(BF16).astype(F32)
                cross = exact_softmax(queries, None, up_keys, up_values)
                joined_ref[pair, rows, :] = (fine + cross + raised[rows, :]).astype(BF16)

    joined = jnp.concatenate([joined_ref[n] for n in range(PAIRS)], 1)
    out_ref[...] = dot(joined, weight_ref[...]).astype(BF16)


def constant(table):
    return jnp.asarray(table, BF16)


def call(kernel, name, outs, operands, flops, hbm=(), scratch=(), vmem=28):
    near = pl.BlockSpec(memory_space=pltpu.VMEM)
    far = pl.BlockSpec(memory_space=pl.ANY)
    moved_bytes = sum(x.size * x.dtype.itemsize for x in list(operands) + list(outs))
    return pl.pallas_call(
        kernel,
        in_specs=[far if n in hbm else near for n in range(len(operands))],
        out_specs=[near] * len(outs),
        out_shape=list(outs),
        scratch_shapes=list(scratch),
        compiler_params=pltpu.CompilerParams(vmem_limit_bytes=vmem << 20),
        cost_estimate=pl.CostEstimate(
            flops=int(flops), bytes_accessed=int(moved_bytes), transcendentals=int(flops / 1000)
        ),
        name=name,
    )(*operands)


def shards(fine_query, fine_keyval, coarse_query, coarse_keyval, out_weight):
    channels = fine_query.shape[-1]
    lat, lon = lax.axis_size("lat"), lax.axis_size("lon")
    east = [(i, (i + 1) % lon) for i in range(lon)]
    west = [(b, a) for a, b in east]
    south = [(i, i + 1) for i in range(lat - 1)]
    north = [(b, a) for a, b in south]
    cells = ROWS * COLS
    fq = fine_query.reshape(cells, channels)
    fkv = fine_keyval.reshape(cells, 2 * channels)
    cq = coarse_query.reshape(-1, channels)
    ckv = coarse_keyval.reshape(-1, 2 * channels)
    half = lambda rows: jax.ShapeDtypeStruct((rows, channels), BF16)
    full = lambda rows: jax.ShapeDtypeStruct((rows, 2 * channels), BF16)
    state = jax.ShapeDtypeStruct((cells, channels), F32)

    coarse_east, coarse_west, fine_east, fine_west = call(
        send_east_west_kernel, "send_lon", [full(48), full(48), full(SIDE), full(SIDE)],
        [fkv, ckv, cq, constant(PICK_FINE), constant(PICK_COARSE), constant(PICK_QUERY)], 5e8,
    )
    coarse_left = lax.ppermute(coarse_east, "lon", east)
    coarse_right = lax.ppermute(coarse_west, "lon", west)
    fine_left = lax.ppermute(fine_east, "lon", east)
    fine_right = lax.ppermute(fine_west, "lon", west)

    mid_rows = EDGE + len(BAND)
    band_south, band_north = call(
        send_band_kernel, "send_band", [full(mid_rows)] * 2, [fkv, ckv, coarse_left, coarse_right], 1e6
    )
    mid_top = lax.ppermute(band_south, "lat", south)
    mid_bottom = lax.ppermute(band_north, "lat", north)

    early = call(
        early_kernel, "early", [state] * 4,
        [fq, fkv, ckv, constant(UP_EARLY), constant(FINE_CHOSEN), constant(OWN_MASK)], 1e10,
    )
    mid_top, mid_bottom, early = lax.optimization_barrier((mid_top, mid_bottom, early))

    (coarse_att,) = call(
        coarse_kernel, "coarse", [half(len(COARSE_QUERIES))],
        [cq, ckv, coarse_left, coarse_right, mid_top, mid_bottom, constant(COARSE_CHOSEN), constant(COARSE_MASK)],
        2e9,
    )
    late_south, late_north = call(
        send_late_kernel, "send_late", [full(LATE_ROWS)] * 2,
        [fine_left, fine_right, coarse_att] + [constant(table) for table in LATE_PICKS], 2e8,
    )
    late_top = lax.ppermute(late_south, "lat", south)
    late_bottom = lax.ppermute(late_north, "lat", north)

    sides = [fine_left, fine_right, mid_top, mid_bottom, ckv, coarse_left, coarse_right]
    fine_mixed, fine_total, cross = call(
        middle_kernel, "middle", [state] * 3,
        [fq, *early, *sides, constant(FINE_CHOSEN), constant(SIDE_MASK), constant(UP_LATE)], 6e9,
    )
    (out,) = call(
        late_kernel, "late", [half(cells)],
        [fq, fine_mixed, fine_total, cross, late_top, late_bottom, coarse_att, constant(FINE_CHOSEN),
         constant(CORNER_MASK), constant(UP_ATT), out_weight, fkv, *sides,
         constant(OWN_MASK), constant(SIDE_MASK), constant(UP_EARLY), constant(UP_LATE)],
        3e9,
        hbm=(11, 19, 20, 21, 22),
        scratch=[
            pltpu.VMEM((PAIRS, cells, LANES), BF16), pltpu.VMEM((8, LANES), F32),
            pltpu.VMEM((cells, 2 * channels), BF16), pltpu.VMEM(OWN_MASK.shape, BF16),
            pltpu.VMEM(SIDE_MASK.shape, BF16), pltpu.VMEM(UP_EARLY.shape, BF16),
            pltpu.VMEM(UP_LATE.shape, BF16), pltpu.SemaphoreType.DMA((5,)),
        ],
    )
    return out.reshape(ROWS, COLS, channels)


def solution(mesh):
    tiled = P("lat", "lon", None)
    return jax.shard_map(
        shards, mesh=mesh, in_specs=(tiled,) * 4 + (P(),), out_specs=tiled, check_vma=False
    )
```

time: 222 us -> 75.8 us (0.34)
  the two profiles are of different devices: /device:TPU:0 before, /device:TPU:18 now
where the time goes in v1:
time: 75.8 us; the launch traced here: 75.1 us
  Pallas kernels  43.7 us (58%)
  starting transfers between devices  17.2 us (23%)
  waiting for transfers between devices  8.15 us (11%)
  local copies, waits for them, and re-layouts  5.68 us (7%)
    pallas_call x7, Pallas kernels, call(): pl.pallas_call(kernel, in_specs=[far if n in hbm else near for n in range...  43.7 us
    ppermute x1, waiting for transfers between devices, shards(): coarse_left = lax.ppermute(coarse_east, 'lon', east)  6.81 us
    unnamed x44, local copies, waits for them, and re-layouts  5.68 us
    ppermute x1, starting transfers between devices, shards(): late_bottom = lax.ppermute(late_north, 'lat', north)  3.77 us
    ppermute x1, starting transfers between devices, shards(): mid_bottom = lax.ppermute(band_north, 'lat', north)  3.64 us
    ppermute x1, starting transfers between devices, shards(): fine_right = lax.ppermute(fine_west, 'lon', west)  2.3 us
    ppermute x1, starting transfers between devices, shards(): mid_top = lax.ppermute(band_south, 'lat', south)  1.92 us
    ppermute x1, starting transfers between devices, shards(): late_top = lax.ppermute(late_south, 'lat', south)  1.92 us
  transfers between devices with their start and end apart: 8, of which 2 were waited for; matrix products, arithmetic and copies ran while one was open for 0% of the time, Pallas kernels for 25%

profile of v1, /device:TPU:18, one launch (start us, length us, event | category | flops | bytes accessed | tf_op | source)
XLA Modules:
  0.0 75.1 jit_solution(15659732704763776755)
XLA Ops:
  0.0 1.4 %copy-done = bf16[24,32,1024]{2,1,0:T(8,128)(2,1)S(1)} copy-done((bf16[24,32,1024]{2,1,0:T(8,128)(2,1)S(1)}, bf16[24,32,1024]{2,1,0:T(8,128)(2,1)}, u32[]{:S(2)}) %copy-start) | copy-done | bytes 1572888
  1.4 0.9 %copy-done.3 = bf16[6,8,1024]{2,1,0:T(8,128)(2,1)S(1)} copy-done((bf16[6,8,1024]{2,1,0:T(8,128)(2,1)S(1)}, bf16[6,8,1024]{2,1,0:T(8,128)(2,1)}, u32[]{:S(2)}) %copy-start.3) | copy-done | bytes 98328
  2.3 1.0 %copy-done.8 = bf16[288,768]{1,0:T(8,128)(2,1)S(1)} copy-done((bf16[288,768]{1,0:T(8,128)(2,1)S(1)}, bf16[288,768]{1,0:T(8,128)(2,1)}, u32[]{:S(2)}) %copy-start.8) | copy-done | bytes 442392
  3.3 0.8 %copy-done.17 = bf16[6,8,512]{2,1,0:T(8,128)(2,1)S(1)} copy-done((bf16[6,8,512]{2,1,0:T(8,128)(2,1)S(1)}, bf16[6,8,512]{2,1,0:T(8,128)(2,1)}, u32[]{:S(2)}) %copy-start.17) | copy-done | bytes 49176
  4.1 0.7 copy-done.18
  4.9 0.7 copy-done.19
  5.6 0.0 copy-start.14
  5.6 0.7 send_lon.1
  6.3 1.6 %collective-permute-start = (bf16[48,1024]{1,0:T(8,128)(2,1)S(1)}, bf16[48,1024]{1,0:T(8,128)(2,1)S(1)}, u32[]{:S(2)}, u32[]{:S(2)}) collective-permute-start(bf16[48,1024]{1,0:T(8,128)(2,1)S(1)} %get-tuple-element.26), channel_id=1, source_target_pairs={{0,1},{1,2},{2,3},{3,4},{4,5},{5,6},{6,7},{7,0},{8,9},{9,10},{10,1... | collective-permute-start | bytes 294920 | tf_op jit(solution)/shard_map/ppermute | solution.py:577
  7.9 1.4 %collective-permute-start.1 = (bf16[48,1024]{1,0:T(8,128)(2,1)S(1)}, bf16[48,1024]{1,0:T(8,128)(2,1)S(1)}, u32[]{:S(2)}, u32[]{:S(2)}) collective-permute-start(bf16[48,1024]{1,0:T(8,128)(2,1)S(1)} %get-tuple-element.27), channel_id=1, source_target_pairs={{1,0},{2,1},{3,2},{4,3},{5,4},{6,5},{7,6},{0,7},{9,8},{10,9},{11,1... | collective-permute-start | bytes 294920 | tf_op jit(solution)/shard_map/ppermute | solution.py:578
  9.3 0.6 collective-permute-start.4
  9.9 2.3 %collective-permute-start.5 = (bf16[144,1024]{1,0:T(8,128)(2,1)S(1)}, bf16[144,1024]{1,0:T(8,128)(2,1)S(1)}, u32[]{:S(2)}, u32[]{:S(2)}) collective-permute-start(bf16[144,1024]{1,0:T(8,128)(2,1)S(1)} %get-tuple-element.39), channel_id=1, source_target_pairs={{1,0},{2,1},{3,2},{4,3},{5,4},{6,5},{7,6},{0,7},{9,8},{10,9},{11,1... | collective-permute-start | bytes 884744 | tf_op jit(solution)/shard_map/ppermute | solution.py:580
  12.2 6.8 %collective-permute-done.left_ref.cl_ref = bf16[48,1024]{1,0:T(8,128)(2,1)S(1)} collective-permute-done((bf16[48,1024]{1,0:T(8,128)(2,1)S(1)}, bf16[48,1024]{1,0:T(8,128)(2,1)S(1)}, u32[]{:S(2)}, u32[]{:S(2)}) %collective-permute-start) | collective-permute-done | bytes 98336 | tf_op jit(solution)/shard_map/ppermute | solution.py:577
  19.0 1.3 %collective-permute-done.1.right_ref.cr_ref = bf16[48,1024]{1,0:T(8,128)(2,1)S(1)} collective-permute-done((bf16[48,1024]{1,0:T(8,128)(2,1)S(1)}, bf16[48,1024]{1,0:T(8,128)(2,1)S(1)}, u32[]{:S(2)}, u32[]{:S(2)}) %collective-permute-start.1) | collective-permute-done | bytes 98336 | tf_op jit(solution)/shard_map/ppermute | solution.py:578
  20.3 0.1 send_band.1
  20.4 1.9 %collective-permute-start.2 = (bf16[336,1024]{1,0:T(8,128)(2,1)S(1)}, bf16[336,1024]{1,0:T(8,128)(2,1)S(1)}, u32[]{:S(2)}, u32[]{:S(2)}) collective-permute-start(bf16[336,1024]{1,0:T(8,128)(2,1)S(1)} %get-tuple-element.28), channel_id=1, source_target_pairs={{0,8},{8,16},{16,24},{1,9},{9,17},{17,25},{2,10},{10,18},{18,26},{... | collective-permute-start | bytes 2064392 | tf_op jit(solution)/shard_map/ppermute | solution.py:586
  22.4 3.6 %collective-permute-start.3 = (bf16[336,1024]{1,0:T(8,128)(2,1)S(1)}, bf16[336,1024]{1,0:T(8,128)(2,1)S(1)}, u32[]{:S(2)}, u32[]{:S(2)}) collective-permute-start(bf16[336,1024]{1,0:T(8,128)(2,1)S(1)} %get-tuple-element.29), channel_id=1, source_target_pairs={{8,0},{16,8},{24,16},{9,1},{17,9},{25,17},{10,2},{18,10},{26,18},{... | collective-permute-start | bytes 2064392 | tf_op jit(solution)/shard_map/ppermute | solution.py:587
  26.1 0.0 copy-start.20
  26.1 0.0 copy-start.21
  26.1 8.5 %early.1 = (f32[768,512]{1,0:T(8,128)S(1)}, f32[768,512]{1,0:T(8,128)S(1)}, f32[768,512]{1,0:T(8,128)S(1)}, f32[768,512]{1,0:T(8,128)S(1)}) custom-call(bf16[768,512]{1,0:T(8,128)(2,1)S(1)} %bitcast.15, bf16[768,1024]{1,0:T(8,128)(2,1)S(1)} %bitcast.7, bf16[48,1024]{1,0:T(8,128)(2,1)S(1)} %bitcast.11, bf16[512,48]{1,0:T(8,128)(2,1)S(1)} %copy-done.11, ...), custom_call_target="tpu_custom_call" | custom-call | flops 10000000000 | bytes 9256960 | tf_op jit(solution)/shard_map/early/pallas_call | solution.py:543
  34.6 0.0 copy-start.12
  34.7 0.0 copy-start.13
  34.7 0.0 copy-start.16
  34.7 0.0 copy-start.6
  34.7 0.0 copy-start.10
  34.7 3.2 %coarse.1.att_ref = bf16[80,512]{1,0:T(8,128)(2,1)S(1)} custom-call(bf16[48,512]{1,0:T(8,128)(2,1)S(1)} %bitcast.19, bf16[48,1024]{1,0:T(8,128)(2,1)S(1)} %bitcast.12, bf16[48,1024]{1,0:T(8,128)(2,1)S(1)} %collective-permute-done.left_ref.cl_ref, bf16[48,1024]{1,0:T(8,128)(2,1)S(1)} %collective-permute-done.1.right_ref.cr_ref, ...), custom_call_target="tpu_custom_call" | custom-call | flops 2000000000 | bytes 1953792 | tf_op jit(solution)/shard_map/coarse/pallas_call | solution.py:543
  38.0 0.4 send_late.1
  38.4 1.9 %collective-permute-start.6 = (bf16[96,1024]{1,0:T(8,128)(2,1)S(1)}, bf16[96,1024]{1,0:T(8,128)(2,1)S(1)}, u32[]{:S(2)}, u32[]{:S(2)}) collective-permute-start(bf16[96,1024]{1,0:T(8,128)(2,1)S(1)} %get-tuple-element.45), channel_id=1, source_target_pairs={{0,8},{8,16},{16,24},{1,9},{9,17},{17,25},{2,10},{10,18},{18,26},{... | collective-permute-start | bytes 589832 | tf_op jit(solution)/shard_map/ppermute | solution.py:604
  40.3 0.0 copy-start.15
  40.3 3.8 %collective-permute-start.7 = (bf16[96,1024]{1,0:T(8,128)(2,1)S(1)}, bf16[96,1024]{1,0:T(8,128)(2,1)S(1)}, u32[]{:S(2)}, u32[]{:S(2)}) collective-permute-start(bf16[96,1024]{1,0:T(8,128)(2,1)S(1)} %get-tuple-element.46), channel_id=1, source_target_pairs={{8,0},{16,8},{24,16},{9,1},{17,9},{25,17},{10,2},{18,10},{26,18},{... | collective-permute-start | bytes 589832 | tf_op jit(solution)/shard_map/ppermute | solution.py:605
  44.1 7.1 %middle.1 = (f32[768,512]{1,0:T(8,128)S(1)}, f32[768,512]{1,0:T(8,128)S(1)}, f32[768,512]{1,0:T(8,128)S(1)}) custom-call(bf16[768,512]{1,0:T(8,128)(2,1)S(1)} %bitcast.16, f32[768,512]{1,0:T(8,128)S(1)} %get-tuple-element.34.of_ref, f32[768,512]{1,0:T(8,128)S(1)} %get-tuple-element.35.lf_ref, f32[768,512]{1,0:T(8,128)S(1)} %get-tuple-element.36.oc_ref, ...), custom_call_target="tpu_custom_call" | custom-call | flops 6000000000 | bytes 15187968 | tf_op jit(solution)/shard_map/middle/pallas_call | solution.py:543
  51.3 23.8 %late.1 = bf16[768,512]{1,0:T(8,128)(2,1)} custom-call(bf16[768,512]{1,0:T(8,128)(2,1)S(1)} %bitcast.17, f32[768,512]{1,0:T(8,128)S(1)} %get-tuple-element.42.fo_ref, f32[768,512]{1,0:T(8,128)S(1)} %get-tuple-element.43.fl_ref, f32[768,512]{1,0:T(8,128)S(1)} %get-tuple-element.44.cross_ref, bf16[96,1024]{1,0:T(8,128)(2,1)S(1)} %collective-permute-done.6.lt_ref, ...), custom_call_target="tpu_custom_call" | custom-call | flops 3000000000 | bytes 13410304 | tf_op jit(solution)/shard_map/late/pallas_call | solution.py:543
  (35 shorter events, 0.1 us)
Async XLA Ops:
  0.0 1.4 %copy-start = (bf16[24,32,1024]{2,1,0:T(8,128)(2,1)S(1)}, bf16[24,32,1024]{2,1,0:T(8,128)(2,1)}, u32[]{:S(2)}) copy-start(bf16[24,32,1024]{2,1,0:T(8,128)(2,1)} %param.27) | copy-start | bytes 4718596
  1.4 0.9 %copy-start.3 = (bf16[6,8,1024]{2,1,0:T(8,128)(2,1)S(1)}, bf16[6,8,1024]{2,1,0:T(8,128)(2,1)}, u32[]{:S(2)}) copy-start(bf16[6,8,1024]{2,1,0:T(8,128)(2,1)} %param.29) | copy-start | bytes 294916
  2.3 1.0 %copy-start.8 = (bf16[288,768]{1,0:T(8,128)(2,1)S(1)}, bf16[288,768]{1,0:T(8,128)(2,1)}, u32[]{:S(2)}) copy-start(bf16[288,768]{1,0:T(8,128)(2,1)} %constant.30.clone.pf_ref) | copy-start | bytes 1327108
  3.3 0.8 %copy-start.17 = (bf16[6,8,512]{2,1,0:T(8,128)(2,1)S(1)}, bf16[6,8,512]{2,1,0:T(8,128)(2,1)}, u32[]{:S(2)}) copy-start(bf16[6,8,512]{2,1,0:T(8,128)(2,1)} %param.28) | copy-start | bytes 147460
  4.1 0.7 copy-start.18
  4.9 0.7 copy-start.19
  5.6 20.4 %copy-start.1 = (bf16[24,32,1024]{2,1,0:T(8,128)(2,1)S(1)}, bf16[24,32,1024]{2,1,0:T(8,128)(2,1)}, u32[]{:S(2)}) copy-start(bf16[24,32,1024]{2,1,0:T(8,128)(2,1)} %param.27) | copy-start | bytes 4718596
  5.6 20.4 %copy-start.5 = (bf16[24,32,512]{2,1,0:T(8,128)(2,1)S(1)}, bf16[24,32,512]{2,1,0:T(8,128)(2,1)}, u32[]{:S(2)}) copy-start(bf16[24,32,512]{2,1,0:T(8,128)(2,1)} %param.26) | copy-start | bytes 2359300
  5.6 20.4 %copy-start.9 = (bf16[1536,128]{1,0:T(8,128)(2,1)S(1)}, bf16[1536,128]{1,0:T(8,128)(2,1)}, u32[]{:S(2)}) copy-start(bf16[1536,128]{1,0:T(8,128)(2,1)} %constant.35.clone.mask_ref.own_mask_hbm) | copy-start | bytes 1179652
  5.6 20.4 %copy-start.11 = (bf16[512,48]{1,0:T(8,128)(2,1)S(1)}, bf16[512,48]{1,0:T(8,128)(2,1)}, u32[]{:S(2)}) copy-start(bf16[512,48]{1,0:T(8,128)(2,1)} %constant.33.clone.up_ref.early_hbm) | copy-start | bytes 147460
  5.6 20.5 %copy-start.14 = (bf16[256,128]{1,0:T(8,128)(2,1)S(1)}, bf16[256,128]{1,0:T(8,128)(2,1)}, u32[]{:S(2)}) copy-start(bf16[256,128]{1,0:T(8,128)(2,1)} %constant.34.clone.chosen_ref) | copy-start | bytes 196612
  6.3 12.7 %collective-permute-start = (bf16[48,1024]{1,0:T(8,128)(2,1)S(1)}, bf16[48,1024]{1,0:T(8,128)(2,1)S(1)}, u32[]{:S(2)}, u32[]{:S(2)}) collective-permute-start(bf16[48,1024]{1,0:T(8,128)(2,1)S(1)} %get-tuple-element.26), channel_id=1, source_target_pairs={{0,1},{1,2},{2,3},{3,4},{4,5},{5,6},{6,7},{7,0},{8,9},{9,10},{10,1... | collective-permute-start | bytes 294920 | tf_op jit(solution)/shard_map/ppermute | solution.py:577
  7.9 12.5 %collective-permute-start.1 = (bf16[48,1024]{1,0:T(8,128)(2,1)S(1)}, bf16[48,1024]{1,0:T(8,128)(2,1)S(1)}, u32[]{:S(2)}, u32[]{:S(2)}) collective-permute-start(bf16[48,1024]{1,0:T(8,128)(2,1)S(1)} %get-tuple-element.27), channel_id=1, source_target_pairs={{1,0},{2,1},{3,2},{4,3},{5,4},{6,5},{7,6},{0,7},{9,8},{10,9},{11,1... | collective-permute-start | bytes 294920 | tf_op jit(solution)/shard_map/ppermute | solution.py:578
  9.3 28.6 %collective-permute-start.4 = (bf16[144,1024]{1,0:T(8,128)(2,1)S(1)}, bf16[144,1024]{1,0:T(8,128)(2,1)S(1)}, u32[]{:S(2)}, u32[]{:S(2)}) collective-permute-start(bf16[144,1024]{1,0:T(8,128)(2,1)S(1)} %get-tuple-element.38), channel_id=1, source_target_pairs={{0,1},{1,2},{2,3},{3,4},{4,5},{5,6},{6,7},{7,0},{8,9},{9,10},{10,1... | collective-permute-start | bytes 884744 | tf_op jit(solution)/shard_map/ppermute | solution.py:579
  9.9 28.0 %collective-permute-start.5 = (bf16[144,1024]{1,0:T(8,128)(2,1)S(1)}, bf16[144,1024]{1,0:T(8,128)(2,1)S(1)}, u32[]{:S(2)}, u32[]{:S(2)}) collective-permute-start(bf16[144,1024]{1,0:T(8,128)(2,1)S(1)} %get-tuple-element.39), channel_id=1, source_target_pairs={{1,0},{2,1},{3,2},{4,3},{5,4},{6,5},{7,6},{0,7},{9,8},{10,9},{11,1... | collective-permute-start | bytes 884744 | tf_op jit(solution)/shard_map/ppermute | solution.py:580
  20.4 14.2 %collective-permute-start.2 = (bf16[336,1024]{1,0:T(8,128)(2,1)S(1)}, bf16[336,1024]{1,0:T(8,128)(2,1)S(1)}, u32[]{:S(2)}, u32[]{:S(2)}) collective-permute-start(bf16[336,1024]{1,0:T(8,128)(2,1)S(1)} %get-tuple-element.28), channel_id=1, source_target_pairs={{0,8},{8,16},{16,24},{1,9},{9,17},{17,25},{2,10},{10,18},{18,26},{... | collective-permute-start | bytes 2064392 | tf_op jit(solution)/shard_map/ppermute | solution.py:586
  22.4 12.2 %collective-permute-start.3 = (bf16[336,1024]{1,0:T(8,128)(2,1)S(1)}, bf16[336,1024]{1,0:T(8,128)(2,1)S(1)}, u32[]{:S(2)}, u32[]{:S(2)}) collective-permute-start(bf16[336,1024]{1,0:T(8,128)(2,1)S(1)} %get-tuple-element.29), channel_id=1, source_target_pairs={{8,0},{16,8},{24,16},{9,1},{17,9},{25,17},{10,2},{18,10},{26,18},{... | collective-permute-start | bytes 2064392 | tf_op jit(solution)/shard_map/ppermute | solution.py:587
  26.1 8.6 %copy-start.4 = (bf16[6,8,1024]{2,1,0:T(8,128)(2,1)S(1)}, bf16[6,8,1024]{2,1,0:T(8,128)(2,1)}, u32[]{:S(2)}) copy-start(bf16[6,8,1024]{2,1,0:T(8,128)(2,1)} %param.29) | copy-start | bytes 294916
  26.1 8.6 %copy-start.20 = (bf16[512,128]{1,0:T(8,128)(2,1)S(1)}, bf16[512,128]{1,0:T(8,128)(2,1)}, u32[]{:S(2)}) copy-start(bf16[512,128]{1,0:T(8,128)(2,1)} %constant.37.clone.mask_ref) | copy-start | bytes 393220
  26.1 8.6 %copy-start.21 = (bf16[80,128]{1,0:T(8,128)(2,1)S(1)}, bf16[80,128]{1,0:T(8,128)(2,1)}, u32[]{:S(2)}) copy-start(bf16[80,128]{1,0:T(8,128)(2,1)} %constant.36.clone.chosen_ref) | copy-start | bytes 61444
  34.6 3.3 %copy-start.12 = (bf16[192,144]{1,0:T(8,128)(2,1)S(1)}, bf16[192,144]{1,0:T(8,128)(2,1)}, u32[]{:S(2)}) copy-start(bf16[192,144]{1,0:T(8,128)(2,1)} %constant.39.clone.pr_ref) | copy-start | bytes 165892
  34.7 3.3 %copy-start.13 = (bf16[192,144]{1,0:T(8,128)(2,1)S(1)}, bf16[192,144]{1,0:T(8,128)(2,1)}, u32[]{:S(2)}) copy-start(bf16[192,144]{1,0:T(8,128)(2,1)} %constant.38.clone.pl_ref) | copy-start | bytes 165892
  34.7 3.3 %copy-start.16 = (bf16[192,80]{1,0:T(8,128)(2,1)S(1)}, bf16[192,80]{1,0:T(8,128)(2,1)}, u32[]{:S(2)}) copy-start(bf16[192,80]{1,0:T(8,128)(2,1)} %constant.40.clone.pa_ref) | copy-start | bytes 92164
  34.7 9.4 %copy-start.6 = (bf16[3,256,512]{2,1,0:T(8,128)(2,1)S(1)}, bf16[3,256,512]{2,1,0:T(8,128)(2,1)}, u32[]{:S(2)}) copy-start(bf16[3,256,512]{2,1,0:T(8,128)(2,1)} %constant.42.clone.late_ref.late_hbm) | copy-start | bytes 2359300
  34.7 9.4 %copy-start.10 = (bf16[1088,128]{1,0:T(8,128)(2,1)S(1)}, bf16[1088,128]{1,0:T(8,128)(2,1)}, u32[]{:S(2)}) copy-start(bf16[1088,128]{1,0:T(8,128)(2,1)} %constant.41.clone.mask_ref.side_mask_hbm) | copy-start | bytes 835588
  38.4 12.9 %collective-permute-start.6 = (bf16[96,1024]{1,0:T(8,128)(2,1)S(1)}, bf16[96,1024]{1,0:T(8,128)(2,1)S(1)}, u32[]{:S(2)}, u32[]{:S(2)}) collective-permute-start(bf16[96,1024]{1,0:T(8,128)(2,1)S(1)} %get-tuple-element.45), channel_id=1, source_target_pairs={{0,8},{8,16},{16,24},{1,9},{9,17},{17,25},{2,10},{10,18},{18,26},{... | collective-permute-start | bytes 589832 | tf_op jit(solution)/shard_map/ppermute | solution.py:604
  40.3 10.9 %copy-start.2 = (bf16[3,768,144]{2,1,0:T(8,128)(2,1)S(1)}, bf16[3,768,144]{2,1,0:T(8,128)(2,1)}, u32[]{:S(2)}) copy-start(bf16[3,768,144]{2,1,0:T(8,128)(2,1)} %constant.44.clone.up_ref) | copy-start | bytes 1990660
  40.3 10.9 %copy-start.7 = (bf16[512,512]{1,0:T(8,128)(2,1)S(1)}, bf16[512,512]{1,0:T(8,128)(2,1)}, u32[]{:S(2)}) copy-start(bf16[512,512]{1,0:T(8,128)(2,1)} %weight_ref.1) | copy-start | bytes 1572868
  40.3 10.9 %copy-start.15 = (bf16[192,128]{1,0:T(8,128)(2,1)S(1)}, bf16[192,128]{1,0:T(8,128)(2,1)}, u32[]{:S(2)}) copy-start(bf16[192,128]{1,0:T(8,128)(2,1)} %constant.43.clone.mask_ref) | copy-start | bytes 147460
  40.3 10.9 %collective-permute-start.7 = (bf16[96,1024]{1,0:T(8,128)(2,1)S(1)}, bf16[96,1024]{1,0:T(8,128)(2,1)S(1)}, u32[]{:S(2)}, u32[]{:S(2)}) collective-permute-start(bf16[96,1024]{1,0:T(8,128)(2,1)S(1)} %get-tuple-element.46), channel_id=1, source_target_pairs={{8,0},{16,8},{24,16},{9,1},{17,9},{25,17},{10,2},{18,10},{26,18},{... | collective-permute-start | bytes 589832 | tf_op jit(solution)/shard_map/ppermute | solution.py:605

commit v2 on v1

v2 whole, which is shorter than its diff:
```python
import math

import jax
import jax.numpy as jnp
import numpy as np
from jax import lax
from jax.experimental import pallas as pl
from jax.experimental.pallas import tpu as pltpu
from jax.sharding import PartitionSpec as P

HEADS = 8
RADIUS = 6
FACTOR = 4
ROWS, COLS = 24, 32
CROWS, CCOLS = 6, 8
LANES = 128
BLOCK_ROWS = 8
BLOCKS = ROWS // BLOCK_ROWS
BLOCK = BLOCK_ROWS * COLS
MASKED = -16384.0
EXPONENT = 0.125 * math.log2(math.e)
F32 = jnp.float32
BF16 = jnp.bfloat16


ROW_ORDER = list(range(2, 22)) + [0, 1, 22, 23]
LEFT_FINE = [(r, c - RADIUS) for r in ROW_ORDER for c in range(RADIUS)]
RIGHT_FINE = [(r, COLS + c) for r in ROW_ORDER for c in range(RADIUS)]
CORNER_TOP = list(range(0, 24)) + list(range(120, 132))
CORNER_BOTTOM = list(range(96, 120)) + list(range(132, 144))
CORNERS = 36
LATE_ROWS = 96


OWN_BLOCKS = [((0, 10), (0, 16)), ((10, 14), (4, 20)), ((14, 24), (8, 24))]


def corner_keys(top):
    picks = CORNER_BOTTOM if top else CORNER_TOP
    shift = -ROWS if top else ROWS
    keys = [(LEFT_FINE[i][0] + shift, LEFT_FINE[i][1]) for i in picks]
    keys += [(RIGHT_FINE[i][0] + shift, RIGHT_FINE[i][1]) for i in picks]
    return keys + [None] * (LATE_ROWS - len(keys))


def mask_lanes(keys, rows, cols):
    table = np.zeros((len(keys), LANES), np.float32)
    for n, key in enumerate(keys):
        if key is None:
            table[n, : len(rows) + len(cols)] = MASKED
            continue
        for i, row in enumerate(rows):
            if abs(key[0] - row) > RADIUS:
                table[n, i] = MASKED
        for j, col in enumerate(cols):
            if abs(key[1] - col) > RADIUS:
                table[n, len(rows) + j] = MASKED
    return table


def chosen_lanes(queries, rows, cols):
    table = np.zeros((len(queries), LANES), np.float32)
    for n, query in enumerate(queries):
        if query is None:
            continue
        table[n, rows.index(query[0])] = 1.0
        table[n, len(rows) + cols.index(query[1])] = 1.0
        table[n, LANES - 1] = 1.0
    return table


def cells_of(rows, cols):
    return [(r, c) for r in rows for c in cols]


FINE_COLS = list(range(COLS))
EDGE = RADIUS * COLS
GROUP = 8
WEST_COLS, EAST_COLS = list(range(GROUP)), list(range(COLS - GROUP, COLS))
ALL_ROWS = list(range(ROWS))
TOP_ROWS, BOTTOM_ROWS = list(range(RADIUS)), list(range(ROWS - RADIUS, ROWS))
TOP_FINE = cells_of(range(-RADIUS, 0), range(COLS))
BOTTOM_FINE = cells_of(range(ROWS, ROWS + RADIUS), range(COLS))
OWN_FINE = cells_of(ALL_ROWS, FINE_COLS)


def tables_of(queries, keys):
    rows = sorted({q[0] for q in queries})
    cols = sorted({q[1] for q in queries})
    return chosen_lanes(queries, rows, cols), mask_lanes(keys, rows, cols)


def stacked(pairs):
    made = [tables_of(*pair) for pair in pairs]
    return [np.concatenate(tables) for tables in zip(*made)]


OWN_CHOSEN, OWN_MASK = stacked(
    [
        (cells_of(range(*q), FINE_COLS), cells_of(range(*k), FINE_COLS))
        for q, k in OWN_BLOCKS
    ]
)
LON_CHOSEN, LON_MASK = stacked(
    [
        (cells_of(ALL_ROWS, WEST_COLS), LEFT_FINE),
        (cells_of(ALL_ROWS, EAST_COLS), RIGHT_FINE),
    ]
)
LAT_CHOSEN, LAT_MASK = stacked(
    [
        (cells_of(TOP_ROWS, FINE_COLS), TOP_FINE),
        (cells_of(BOTTOM_ROWS, FINE_COLS), BOTTOM_FINE),
    ]
)
CORNER_CHOSEN, CORNER_MASK = stacked(
    [
        (cells_of(TOP_ROWS, WEST_COLS) + cells_of(TOP_ROWS, EAST_COLS), corner_keys(True)),
        (cells_of(BOTTOM_ROWS, WEST_COLS) + cells_of(BOTTOM_ROWS, EAST_COLS), corner_keys(False)),
    ]
)
EXACT_KEYS = (
    OWN_FINE + LEFT_FINE + RIGHT_FINE + TOP_FINE + corner_keys(True) + BOTTOM_FINE + corner_keys(False)
)
EXACT_CHOSEN, EXACT_MASK = stacked(
    [
        (cells_of(range(b * BLOCK_ROWS, (b + 1) * BLOCK_ROWS), FINE_COLS), EXACT_KEYS)
        for b in range(BLOCKS)
    ]
)

CQ_COLS = list(range(-1, CCOLS + 1))
OWN_COARSE = [(r, c) for r in range(CROWS) for c in range(CCOLS)]
LEFT_COARSE = [(r, c - 7) for r in range(CROWS) for c in range(7)] + [None] * CROWS
RIGHT_COARSE = [(r, c + CCOLS) for r in range(CROWS) for c in range(7)] + [None] * CROWS
BAND = OWN_COARSE + LEFT_COARSE + RIGHT_COARSE


def moved(keys, rows):
    return [None if key is None else (key[0] + rows, key[1]) for key in keys]


COARSE_KEYS = BAND + moved(BAND, -CROWS) + moved(BAND, CROWS)
COARSE_COUNT = 512
COARSE_KEYS = COARSE_KEYS + [None] * (COARSE_COUNT - len(COARSE_KEYS))
COARSE_QUERIES = (
    OWN_COARSE
    + [None] * 10
    + [(r, -1) for r in range(CROWS)]
    + [None] * 10
    + [(r, CCOLS) for r in range(CROWS)]
)
COARSE_CHOSEN = chosen_lanes(COARSE_QUERIES, list(range(CROWS)), CQ_COLS)
COARSE_MASK = mask_lanes(COARSE_KEYS, list(range(CROWS)), CQ_COLS)
LATE_ATT = (
    [None] * 8
    + [(0, c) for c in range(CCOLS)]
    + [(0, -1), (0, CCOLS)]
    + [None] * (LATE_ROWS - 2 * CORNERS - 10)
)
ATT_CELLS = COARSE_QUERIES + moved(LATE_ATT, -1) + moved(LATE_ATT, CROWS)


def coefficient(fine):
    coarse, offset = fine // FACTOR, (fine % FACTOR - 1.5) / FACTOR
    taps = {coarse: 1.0 - abs(offset)}
    taps[coarse + (1 if offset > 0 else -1)] = abs(offset)
    return taps


def up_table(fine_cells, coarse_cells, pole):
    where = {cell: n for n, cell in reversed(list(enumerate(coarse_cells))) if cell is not None}
    table = np.zeros((len(fine_cells), len(coarse_cells)), np.float32)
    for n, (row, col) in enumerate(fine_cells):
        for r, a in coefficient(row).items():
            if pole == "top":
                r = max(r, 0)
            if pole == "bottom":
                r = min(r, CROWS - 1)
            for c, b in coefficient(col).items():
                table[n, where[(r, c)]] += a * b
    return table


def poles(fine_cells, coarse_cells):
    return np.stack([up_table(fine_cells, coarse_cells, p) for p in ("none", "top", "bottom")])


FINE_CELLS = [(r, c) for r in range(ROWS) for c in range(COLS)]
INNER = [(r, c) for r in range(2, ROWS - 2) for c in range(2, COLS - 2)]
EARLY_COUNT = 512
EARLY_CELLS = INNER[:EARLY_COUNT]
LATE_CELLS = [cell for cell in FINE_CELLS if cell not in set(EARLY_CELLS)]
UP_EARLY = up_table(EARLY_CELLS, OWN_COARSE, "none")
UP_LATE = poles(LATE_CELLS, COARSE_KEYS)
UP_ATT = poles(FINE_CELLS, ATT_CELLS)


def picked(indices, count):
    table = np.zeros((len(indices), count), np.float32)
    for n, index in enumerate(indices):
        if index is not None:
            table[n, index] = 1.0
    return table


FINE_EAST = [r * COLS + COLS - RADIUS + c for r in ROW_ORDER for c in range(RADIUS)]
FINE_WEST = [r * COLS + c for r in ROW_ORDER for c in range(RADIUS)]
PICK_FINE = picked(FINE_EAST + FINE_WEST, ROWS * COLS)
PICK_COARSE = picked(
    [r * CCOLS + 1 + c for r in range(CROWS) for c in range(7)]
    + [None] * CROWS
    + [r * CCOLS + c for r in range(CROWS) for c in range(7)]
    + [None] * CROWS,
    CROWS * CCOLS,
)
PICK_QUERY = picked(
    [None] * 42
    + [r * CCOLS + CCOLS - 1 for r in range(CROWS)]
    + [None] * 42
    + [r * CCOLS for r in range(CROWS)],
    CROWS * CCOLS,
)
SIDE = len(ROW_ORDER) * RADIUS


def late_picks(corner, row):
    rest = LATE_ROWS - 2 * CORNERS
    left = picked(list(corner) + [None] * (CORNERS + rest), SIDE)
    right = picked([None] * CORNERS + list(corner) + [None] * rest, SIDE)
    cells = [(row, c) for c in range(CCOLS)] + [(row, -1), (row, CCOLS)]
    att = [None] * (2 * CORNERS) + [COARSE_QUERIES.index(cell) for cell in cells]
    att = picked(att + [None] * (LATE_ROWS - len(att)), len(COARSE_QUERIES))
    return left, right, att


LATE_PICKS = [
    np.concatenate(tables)
    for tables in zip(late_picks(CORNER_BOTTOM, CROWS - 1), late_picks(CORNER_TOP, 0))
]


PAIRS = HEADS // 2
LEAST, MOST = 2.0**-80, 2.0**100


def halves():
    return lax.broadcasted_iota(jnp.int32, (1, LANES), 1) < LANES // 2


def head_of(pair, head):
    return jnp.where(halves() == (head == 0), pair, jnp.zeros((), pair.dtype))


def packed(first, second):
    return jnp.where(halves(), first, second)


def dot(a, b):
    return jnp.dot(a, b, preferred_element_type=F32)


def scores(queries, keys):
    return lax.dot_general(queries, keys, (((1,), (1,)), ((), ())), preferred_element_type=F32)


def mix(weights, values):
    mixed = dot(weights.astype(BF16), values)
    return mixed[:, :LANES], mixed[:, LANES:]


def with_ones(values):
    return jnp.concatenate([values, jnp.ones_like(values)], 1)


def even(axis):
    return lax.axis_index(axis) % 2 == 0


def pole_flags():
    lat = lax.axis_index("lat")
    return lat == 0, lat == lax.axis_size("lat") - 1


def pole_table():
    is_top, is_bottom = pole_flags()
    return jnp.where(is_top, 1, jnp.where(is_bottom, 2, 0))


def lanes_of(group):
    if isinstance(group, int):
        return slice(group * LANES, (group + 1) * LANES)
    return pl.ds(pl.multiple_of(group * LANES, LANES), LANES)


def low(pair):
    return lanes_of(pair)


def high(pair):
    return lanes_of(pair + PAIRS)


def close_edge(mask, closed):
    lane = lax.broadcasted_iota(jnp.int32, (1, LANES), 1)
    return jnp.where((lane == LANES - 1) & closed, MASKED, mask.astype(F32)).astype(BF16)


def before_after(axis, first, second, *index):
    a, b = first[index], second[index]
    return jnp.where(even(axis), b, a), jnp.where(even(axis), a, b)


def both_heads(queries, chosen):
    rows = jnp.concatenate([head_of(queries, 0), head_of(queries, 1)], 0)
    if chosen is None:
        return rows
    return jnp.concatenate([rows, jnp.concatenate([chosen, chosen], 0)], 1)


def plain_softmax(queries, chosen, keys, values):
    count = queries.shape[0]
    mixed, total = mix(jnp.exp2(scores(both_heads(queries, chosen), keys) * EXPONENT), values)
    return packed(mixed[:count], mixed[count:]), packed(total[:count], total[count:])


def exact_softmax(queries, chosen, keys, values):
    count = queries.shape[0]
    score = scores(both_heads(queries, chosen), keys)
    score = score - jnp.max(score, 1, keepdims=True)
    mixed, total = mix(jnp.exp2(score * EXPONENT), values)
    result = mixed / total
    return packed(result[:count], result[count:])


def settled(mixed, total):
    fits = (total > LEAST) & (total < MOST)
    return jnp.where(fits, mixed / total, jnp.nan)


def fetch(moves, sems):
    copies = [pltpu.make_async_copy(a, b, sems.at[n]) for n, (a, b) in enumerate(moves)]
    for copy in copies:
        copy.start()
    for copy in copies:
        copy.wait()


def send_first_kernel(
    fkv_hbm, ckv_hbm, cq_hbm, pf_hbm, pc_hbm, pq_hbm, c0_ref, c1_ref, f0_ref, f1_ref, r0_ref, r1_ref,
    fkv_ref, ckv_ref, cq_ref, pf_ref, pc_ref, pq_ref, sems,
):
    fetch(
        [(fkv_hbm, fkv_ref), (ckv_hbm, ckv_ref), (cq_hbm, cq_ref),
         (pf_hbm, pf_ref), (pc_hbm, pc_ref), (pq_hbm, pq_ref)],
        sems,
    )
    cells, channels = fkv_ref.shape[0], cq_ref.shape[1]
    eastward = even("lon")
    coarse = dot(pc_ref[...], ckv_ref[...])
    query = dot(pq_ref[...], cq_ref[...])
    coarse = jnp.concatenate([coarse[:, :channels] + query, coarse[:, channels:]], 1).astype(BF16)
    c0_ref[...] = jnp.where(eastward, coarse[:48], coarse[48:])
    c1_ref[...] = jnp.where(eastward, coarse[48:], coarse[:48])
    fine = dot(pf_ref[...], fkv_ref[...]).astype(BF16)
    f0_ref[...] = jnp.where(eastward, fine[:SIDE], fine[SIDE:])
    f1_ref[...] = jnp.where(eastward, fine[SIDE:], fine[:SIDE])
    southward = even("lat")
    last = cells - EDGE
    r0_ref[...] = fkv_ref[pl.ds(pl.multiple_of(jnp.where(southward, last, 0), EDGE), EDGE), :]
    r1_ref[...] = fkv_ref[pl.ds(pl.multiple_of(jnp.where(southward, 0, last), EDGE), EDGE), :]


def send_band_kernel(ckv_ref, c0_ref, c1_ref, band_ref):
    left, right = before_after("lon", c0_ref, c1_ref, slice(None), slice(None))
    band_ref[0:48, :] = ckv_ref[...]
    band_ref[48:96, :] = left
    band_ref[96:144, :] = right


def send_late_kernel(f0_ref, f1_ref, att_ref, pl_ref, pr_ref, pa_ref, l0_ref, l1_ref):
    channels = att_ref.shape[1]
    left, right = before_after("lon", f0_ref, f1_ref, slice(None), slice(None))
    sides = dot(pl_ref[...], left) + dot(pr_ref[...], right)
    att = dot(pa_ref[...], att_ref[...])
    late = jnp.concatenate([sides[:, :channels] + att, sides[:, channels:]], 1).astype(BF16)
    southward = even("lat")
    l0_ref[...] = jnp.where(southward, late[:LATE_ROWS], late[LATE_ROWS:])
    l1_ref[...] = jnp.where(southward, late[LATE_ROWS:], late[:LATE_ROWS])


def own_kernel(q_ref, kv_ref, chosen_ref, mask_ref, mixed_ref, total_ref):
    for pair in range(PAIRS):
        lo, hi = low(pair), high(pair)
        at = 0
        for (q0, q1), (k0, k1) in OWN_BLOCKS:
            rows = slice(q0 * COLS, q1 * COLS)
            near = slice(k0 * COLS, k1 * COLS)
            mask = mask_ref[at : at + (k1 - k0) * COLS, :]
            at += (k1 - k0) * COLS
            keys = jnp.concatenate([kv_ref[near, lo], mask], 1)
            mixed_ref[rows, lo], total_ref[rows, lo] = plain_softmax(
                q_ref[rows, lo], chosen_ref[rows, :], keys, with_ones(kv_ref[near, hi])
            )


def early_cross_kernel(q_ref, ckv_ref, up_ref, mixed_ref, total_ref):
    up = up_ref[...]

    for pair in range(PAIRS):
        lo, hi = low(pair), high(pair)
        up_keys = dot(up, ckv_ref[:, lo]).astype(BF16)
        up_values = with_ones(dot(up, ckv_ref[:, hi]).astype(BF16))
        for block in range(BLOCKS):
            rows = slice(block * BLOCK, (block + 1) * BLOCK)
            mixed_ref[rows, lo], total_ref[rows, lo] = plain_softmax(
                q_ref[rows, lo], None, up_keys, up_values
            )


def columns(queries, first):
    rows = queries.shape[0] // COLS
    split = queries.astype(F32).reshape(rows, COLS, LANES)[:, first : first + GROUP]
    return split.reshape(rows * GROUP, LANES).astype(BF16)


def lon_kernel(q_ref, f0_ref, f1_ref, chosen_ref, mask_ref, mixed_ref, total_ref):
    strip = ROWS * GROUP

    for pair in range(PAIRS):
        lo, hi = low(pair), high(pair)
        side_keys = before_after("lon", f0_ref, f1_ref, slice(None), lo)
        side_values = before_after("lon", f0_ref, f1_ref, slice(None), hi)
        queries = q_ref[:, lo]
        for n, first in enumerate((0, COLS - GROUP)):
            rows = slice(n * strip, (n + 1) * strip)
            keys = jnp.concatenate([side_keys[n], mask_ref[n * SIDE : (n + 1) * SIDE, :]], 1)
            mixed_ref[rows, lo], total_ref[rows, lo] = plain_softmax(
                columns(queries, first), chosen_ref[rows, :], keys, with_ones(side_values[n])
            )


def gathered(own, coarse, band, lanes):
    left, right = before_after("lon", *coarse, slice(None), lanes)
    top, bottom = before_after("lat", *band, slice(None), lanes)
    pad = jnp.zeros((COARSE_COUNT - 3 * len(BAND), LANES), BF16)
    return jnp.concatenate([own[:, lanes], left, right, top, bottom, pad], 0)


def coarse_kernel(q_ref, own_ref, c0_ref, c1_ref, b0_ref, b1_ref, chosen_ref, mask_ref, out_ref):
    is_top, is_bottom = pole_flags()
    band = len(BAND)
    mask = [
        mask_ref[:band, :],
        close_edge(mask_ref[band : 2 * band, :], is_top),
        close_edge(mask_ref[2 * band :, :], is_bottom),
    ]
    mask = jnp.concatenate(mask, 0)
    chosen = chosen_ref[...]
    for pair in range(PAIRS):
        lo = slice(pair * LANES, (pair + 1) * LANES)
        hi = slice((pair + PAIRS) * LANES, (pair + PAIRS + 1) * LANES)
        keys = jnp.concatenate([gathered(own_ref, (c0_ref, c1_ref), (b0_ref, b1_ref), lo), mask], 1)
        values = with_ones(gathered(own_ref, (c0_ref, c1_ref), (b0_ref, b1_ref), hi))
        left, right = before_after("lon", c0_ref, c1_ref, slice(32, 48), lo)
        queries = jnp.concatenate([q_ref[:, lo], left, right], 0)
        out_ref[:, lo] = exact_softmax(queries, chosen, keys, values).astype(BF16)


def middle_kernel(
    q_ref, oc_ref, lc_ref, ckv_ref, c0_ref, c1_ref, b0_ref, b1_ref, r0_ref, r1_ref,
    chosen_ref, mask_ref, late_ref, cross_ref, mixed_ref, total_ref,
):
    cells = q_ref.shape[0]
    late = late_ref[pole_table()]
    closed = pole_flags()
    masks = [close_edge(mask_ref[n * EDGE : (n + 1) * EDGE, :], closed[n]) for n in range(2)]

    for pair in range(PAIRS):
        lo, hi = low(pair), high(pair)
        coarse = (ckv_ref, (c0_ref, c1_ref), (b0_ref, b1_ref))
        up_keys = dot(late, gathered(*coarse, lo)).astype(BF16)
        up_values = with_ones(dot(late, gathered(*coarse, hi)).astype(BF16))
        edge_keys = before_after("lat", r0_ref, r1_ref, slice(None), lo)
        edge_values = before_after("lat", r0_ref, r1_ref, slice(None), hi)
        for n, first in enumerate((0, cells - EDGE)):
            rows = slice(n * EDGE, (n + 1) * EDGE)
            keys = jnp.concatenate([edge_keys[n], masks[n]], 1)
            mixed_ref[rows, lo], total_ref[rows, lo] = plain_softmax(
                q_ref[first : first + EDGE, lo], chosen_ref[rows, :], keys, with_ones(edge_values[n])
            )
        for block in range(BLOCKS):
            rows = slice(block * BLOCK, (block + 1) * BLOCK)
            mixed, total = plain_softmax(q_ref[rows, lo], None, up_keys, up_values)
            cross_ref[rows, lo] = settled(oc_ref[rows, lo] + mixed, lc_ref[rows, lo] + total)


def late_kernel(
    q_ref, of_ref, lf_ref, om_ref, lm_ref, ot_ref, lt_ref, cross_ref, l0_ref, l1_ref, att_ref,
    chosen_ref, mask_ref, up_ref, weight_ref,
    kv_hbm, f0_ref, f1_ref, r0_ref, r1_ref, ckv_ref, c0_ref, c1_ref, b0_ref, b1_ref,
    exact_chosen_hbm, exact_mask_hbm, early_hbm, late_hbm,
    out_ref, joined_ref, bad_ref, mixed_ref, total_ref,
    kv_ref, exact_chosen_ref, exact_mask_ref, early_ref, late_ref, sems,
):
    cells = q_ref.shape[0]
    closed = pole_flags()
    pole = pole_table()
    up = up_ref[pole]
    masks = [close_edge(mask_ref[n * LATE_ROWS : (n + 1) * LATE_ROWS, :], closed[n]) for n in range(2)]
    strip = ROWS * GROUP
    corner = RADIUS * GROUP
    bad_ref[...] = jnp.zeros_like(bad_ref)

    def raised_att(pair):
        top, bottom = before_after("lat", l0_ref, l1_ref, slice(64, 96), low(pair))
        return dot(up, jnp.concatenate([att_ref[:, low(pair)], top, bottom], 0))

    for pair in range(PAIRS):
        lo, hi = low(pair), high(pair)
        corner_keys = before_after("lat", l0_ref, l1_ref, slice(None), lo)
        corner_values = before_after("lat", l0_ref, l1_ref, slice(None), hi)
        raised = raised_att(pair)
        mixed_ref[...], total_ref[...] = of_ref[:, lo], lf_ref[:, lo]
        for n, first in enumerate((0, cells - EDGE)):
            there, here = slice(first, first + EDGE), slice(n * EDGE, (n + 1) * EDGE)
            mixed_ref[there, :] += ot_ref[here, lo]
            total_ref[there, :] += lt_ref[here, lo]
            queries = q_ref[there, lo]
            queries = jnp.concatenate([columns(queries, 0), columns(queries, COLS - GROUP)], 0)
            keys = jnp.concatenate([corner_keys[n], masks[n]], 1)
            chosen = chosen_ref[2 * n * corner : 2 * (n + 1) * corner, :]
            mixed, total = plain_softmax(queries, chosen, keys, with_ones(corner_values[n]))
            for row in range(RADIUS):
                for side, col in enumerate((0, COLS - GROUP)):
                    at = first + row * COLS + col
                    piece = slice(side * corner + row * GROUP, side * corner + (row + 1) * GROUP)
                    mixed_ref[at : at + GROUP, :] += mixed[piece]
                    total_ref[at : at + GROUP, :] += total[piece]
        for row in range(ROWS):
            for side, col in enumerate((0, COLS - GROUP)):
                at = row * COLS + col
                piece = slice(side * strip + row * GROUP, side * strip + (row + 1) * GROUP)
                mixed_ref[at : at + GROUP, :] += om_ref[piece, lo]
                total_ref[at : at + GROUP, :] += lm_ref[piece, lo]
        fine = settled(mixed_ref[...], total_ref[...]).astype(BF16).astype(F32)
        joined = fine + cross_ref[:, lo] + raised
        joined_ref[pair] = joined.astype(BF16)
        bad_ref[...] += jnp.sum(joined.reshape(-1, 8, LANES) * 0.0, 0)

    @pl.when(jnp.logical_not(jnp.sum(bad_ref[...]) == 0.0))
    def _():
        fetch(
            [(kv_hbm, kv_ref), (exact_chosen_hbm, exact_chosen_ref), (exact_mask_hbm, exact_mask_ref),
             (early_hbm, early_ref), (late_hbm, late_ref)],
            sems,
        )
        coarse = (ckv_ref, (c0_ref, c1_ref), (b0_ref, b1_ref))
        early, late = early_ref[...], late_ref[pole]
        count = len(EXACT_KEYS)
        edges = [cells + 2 * SIDE, cells + 2 * SIDE + EDGE + LATE_ROWS, count]

        @pl.loop(0, PAIRS)
        def _(pair):
            def all_of(lanes):
                left, right = before_after("lon", f0_ref, f1_ref, slice(None), lanes)
                top, bottom = before_after("lat", r0_ref, r1_ref, slice(None), lanes)
                late_top, late_bottom = before_after("lat", l0_ref, l1_ref, slice(None), lanes)
                return jnp.concatenate(
                    [kv_ref[:, lanes], left, right, top, late_top, bottom, late_bottom], 0
                )

            def up_of(lanes):
                first = dot(early, ckv_ref[:, lanes]).astype(BF16)
                return jnp.concatenate([first, dot(late, gathered(*coarse, lanes)).astype(BF16)], 0)

            lo, hi = low(pair), high(pair)
            keys, values = all_of(lo), with_ones(all_of(hi))
            up_keys, up_values = up_of(lo), with_ones(up_of(hi))
            raised = raised_att(pair)
            for block in range(BLOCKS):
                mask = exact_mask_ref[block * count : (block + 1) * count, :]
                mask = [mask[: edges[0]]] + [
                    close_edge(mask[edges[n] : edges[n + 1]], closed[n]) for n in range(2)
                ]
                rows = slice(block * BLOCK, (block + 1) * BLOCK)
                queries = q_ref[rows, lo]
                fine = exact_softmax(
                    queries,
                    exact_chosen_ref[rows, :],
                    jnp.concatenate([keys, jnp.concatenate(mask, 0)], 1),
                    values,
                )
                cross = exact_softmax(queries, None, up_keys, up_values)
                joined = fine.astype(BF16).astype(F32) + cross + raised[rows, :]
                joined_ref[pair, rows, :] = joined.astype(BF16)

    joined = jnp.concatenate([joined_ref[n] for n in range(PAIRS)], 1)
    out_ref[...] = dot(joined, weight_ref[...]).astype(BF16)


def constant(table):
    return jnp.asarray(table, BF16)


def call(kernel, name, outs, operands, flops, hbm=(), scratch=(), vmem=28):
    near = pl.BlockSpec(memory_space=pltpu.VMEM)
    far = pl.BlockSpec(memory_space=pltpu.HBM)
    moved_bytes = sum(x.size * x.dtype.itemsize for x in list(operands) + list(outs))
    return pl.pallas_call(
        kernel,
        in_specs=[far if n in hbm else near for n in range(len(operands))],
        out_specs=[near] * len(outs),
        out_shape=list(outs),
        scratch_shapes=list(scratch),
        compiler_params=pltpu.CompilerParams(vmem_limit_bytes=vmem << 20),
        cost_estimate=pl.CostEstimate(
            flops=int(flops), bytes_accessed=int(moved_bytes), transcendentals=int(flops / 1000)
        ),
        name=name,
    )(*operands)


def swaps(array, other, axis, ring):
    size = lax.axis_size(axis)
    first = [(i, i + 1) for i in range(0, size - 1, 2)]
    second = [(i, (i + 1) % size) for i in range(1, size if ring else size - 1, 2)]
    both = lambda pairs: pairs + [(b, a) for a, b in pairs]
    return lax.ppermute(array, axis, both(first)), lax.ppermute(other, axis, both(second))


def shards(fine_query, fine_keyval, coarse_query, coarse_keyval, out_weight):
    channels = fine_query.shape[-1]
    cells = ROWS * COLS
    fq = fine_query.reshape(cells, channels)
    fkv = fine_keyval.reshape(cells, 2 * channels)
    cq = coarse_query.reshape(-1, channels)
    ckv = coarse_keyval.reshape(-1, 2 * channels)
    half = lambda rows: jax.ShapeDtypeStruct((rows, channels), BF16)
    full = lambda rows: jax.ShapeDtypeStruct((rows, 2 * channels), BF16)
    state = lambda rows: jax.ShapeDtypeStruct((rows, channels), F32)
    after = lax.optimization_barrier

    picks = [constant(PICK_FINE), constant(PICK_COARSE), constant(PICK_QUERY)]
    first = [fkv, ckv, cq] + picks
    c0, c1, f0, f1, r0, r1 = call(
        send_first_kernel, "send_first", [full(48)] * 2 + [full(SIDE)] * 2 + [full(EDGE)] * 2, first, 5e8,
        hbm=range(6), scratch=[pltpu.VMEM(x.shape, BF16) for x in first] + [pltpu.SemaphoreType.DMA((6,))], vmem=56,
    )
    coarse = swaps(c0, c1, "lon", True)
    sides = swaps(f0, f1, "lon", True)
    edges = swaps(r0, r1, "lat", False)

    own = call(
        own_kernel, "own", [state(cells)] * 2, [fq, fkv, constant(OWN_CHOSEN), constant(OWN_MASK)], 5e9
    )
    coarse, own = after((coarse, own))
    (band,) = call(send_band_kernel, "send_band", [full(len(BAND))], [ckv, *coarse], 1e6)
    bands = swaps(band, band, "lat", False)

    fq, _ = after((fq, band))
    early = call(early_cross_kernel, "early_cross", [state(cells)] * 2, [fq, ckv, constant(UP_EARLY)], 5e9)
    sides, _ = after((sides, early))
    lon = call(
        lon_kernel, "lon_strips", [state(2 * ROWS * GROUP)] * 2,
        [fq, *sides, constant(LON_CHOSEN), constant(LON_MASK)], 1.5e9,
    )
    bands, _ = after((bands, lon))
    (coarse_att,) = call(
        coarse_kernel, "coarse", [half(len(COARSE_QUERIES))],
        [cq, ckv, *coarse, *bands, constant(COARSE_CHOSEN), constant(COARSE_MASK)], 2e9,
    )
    late0, late1 = call(
        send_late_kernel, "send_late", [full(LATE_ROWS)] * 2,
        [*sides, coarse_att] + [constant(table) for table in LATE_PICKS], 2e8,
    )
    lates = swaps(late0, late1, "lat", False)

    cross, lat_mixed, lat_total = call(
        middle_kernel, "middle", [state(cells), state(2 * EDGE), state(2 * EDGE)],
        [fq, *early, ckv, *coarse, *bands, *edges, constant(LAT_CHOSEN), constant(LAT_MASK), constant(UP_LATE)],
        5e9,
    )
    exact = [constant(table) for table in (EXACT_CHOSEN, EXACT_MASK, UP_EARLY, UP_LATE)]
    (out,) = call(
        late_kernel, "late", [half(cells)],
        [fq, *own, *lon, lat_mixed, lat_total, cross, *lates, coarse_att, constant(CORNER_CHOSEN),
         constant(CORNER_MASK), constant(UP_ATT), out_weight,
         fkv, *sides, *edges, ckv, *coarse, *bands, *exact],
        3e9,
        hbm=(15, 25, 26, 27, 28),
        scratch=[
            pltpu.VMEM((PAIRS, cells, LANES), BF16), pltpu.VMEM((8, LANES), F32),
            pltpu.VMEM((cells, LANES), F32), pltpu.VMEM((cells, LANES), F32),
            pltpu.VMEM((cells, 2 * channels), BF16),
            *[pltpu.VMEM(x.shape, BF16) for x in exact], pltpu.SemaphoreType.DMA((5,)),
        ],
    )
    return out.reshape(ROWS, COLS, channels)


def solution(mesh):
    tiled = P("lat", "lon", None)
    return jax.shard_map(
        shards, mesh=mesh, in_specs=(tiled,) * 4 + (P(),), out_specs=tiled, check_vma=False
    )
```

time: 75.8 us -> 65.5 us (0.86)
  the two profiles are of different devices: /device:TPU:18 before, /device:TPU:21 now
where the time goes in v2:
time: 65.5 us; the launch traced here: 65.3 us
  Pallas kernels  43.2 us (66%)
  starting transfers between devices  19.6 us (30%)
  local copies, waits for them, and re-layouts  1.27 us (2%)
  waiting for transfers between devices  0.66 us (1%)
    pallas_call x9, Pallas kernels, call(): pl.pallas_call(kernel, in_specs=[far if n in hbm else near for n in range...  43.2 us
    ppermute x5, starting transfers between devices, swaps(): lax.ppermute(other, axis, both(second))  17 us
    ppermute x5, starting transfers between devices, swaps(): lax.ppermute(array, axis, both(first))  2.58 us
  transfers between devices with their start and end apart: 10, of which 1 were waited for; matrix products, arithmetic and copies ran while one was open for 0% of the time, Pallas kernels for 21%

profile of v2, /device:TPU:21, one launch (start us, length us, event | category | flops | bytes accessed | tf_op | source)
XLA Modules:
  0.0 65.3 jit_solution(8038103246816346252)
XLA Ops:
  0.0 3.5 %send_first.1 = (bf16[48,1024]{1,0:T(8,128)(2,1)}, bf16[48,1024]{1,0:T(8,128)(2,1)}, bf16[144,1024]{1,0:T(8,128)(2,1)}, bf16[144,1024]{1,0:T(8,128)(2,1)}, bf16[...) custom-call(bf16[768,1024]{1,0:T(8,128)(2,1)} %bitcast.5, bf16[48,1024]{1,0:T(8,128)(2,1)} %bitcast.8, ...), custom_call_target="tpu_custom_call" | custom-call | flops 500000000 | bytes 3753984 | tf_op jit(solution)/shard_map/send_first/pallas_call | solution.py:610
  3.5 0.3 collective-permute-start
  3.8 2.3 %collective-permute-start.1 = (bf16[48,1024]{1,0:T(8,128)(2,1)}, bf16[48,1024]{1,0:T(8,128)(2,1)S(1)}, u32[]{:S(2)}, u32[]{:S(2)}) collective-permute-start(bf16[48,1024]{1,0:T(8,128)(2,1)} %get-tuple-element.32), channel_id=1, source_target_pairs={{1,2},{3,4},{5,6},{7,0},{2,1},{4,3},{6,5},{0,7},{9,10},{11,12},{13... | collective-permute-start | bytes 294920 | tf_op jit(solution)/shard_map/ppermute | solution.py:629
  6.1 1.1 %collective-permute-start.3 = (bf16[144,1024]{1,0:T(8,128)(2,1)}, bf16[144,1024]{1,0:T(8,128)(2,1)S(1)}, u32[]{:S(2)}, u32[]{:S(2)}) collective-permute-start(bf16[144,1024]{1,0:T(8,128)(2,1)} %get-tuple-element.41), channel_id=1, source_target_pairs={{1,2},{3,4},{5,6},{7,0},{2,1},{4,3},{6,5},{0,7},{9,10},{11,12},{13... | collective-permute-start | bytes 884744 | tf_op jit(solution)/shard_map/ppermute | solution.py:629
  7.2 1.8 %collective-permute-start.6 = (bf16[192,1024]{1,0:T(8,128)(2,1)}, bf16[192,1024]{1,0:T(8,128)(2,1)S(1)}, u32[]{:S(2)}, u32[]{:S(2)}) collective-permute-start(bf16[192,1024]{1,0:T(8,128)(2,1)} %get-tuple-element.50), channel_id=1, source_target_pairs={{0,8},{16,24},{8,0},{24,16},{1,9},{17,25},{9,1},{25,17},{2,10},{18... | collective-permute-start | bytes 1179656 | tf_op jit(solution)/shard_map/ppermute | solution.py:629
  9.0 1.1 %copy-done.4 = bf16[24,32,512]{2,1,0:T(8,128)(2,1)S(1)} copy-done((bf16[24,32,512]{2,1,0:T(8,128)(2,1)S(1)}, bf16[24,32,512]{2,1,0:T(8,128)(2,1)}, u32[]{:S(2)}) %copy-start.4) | copy-done | bytes 786456
  10.1 3.6 %own.1 = (f32[768,512]{1,0:T(8,128)S(1)}, f32[768,512]{1,0:T(8,128)S(1)}) custom-call(bf16[768,512]{1,0:T(8,128)(2,1)S(1)} %bitcast.14, bf16[768,1024]{1,0:T(8,128)(2,1)S(1)} %bitcast.6, bf16[768,128]{1,0:T(8,128)(2,1)S(1)} %copy-done.17, bf16[1536,128]{1,0:T(8,128)(2,1)S(1)} %copy-done.16), custom_call_target="tpu_custom_call" | custom-call | flops 5000000000 | bytes 6094848 | tf_op jit(solution)/shard_map/own/pallas_call | solution.py:610
  13.7 7.5 %collective-permute-start.7 = (bf16[192,1024]{1,0:T(8,128)(2,1)S(1)}, bf16[192,1024]{1,0:T(8,128)(2,1)S(1)}, u32[]{:S(2)}, u32[]{:S(2)}) collective-permute-start(bf16[192,1024]{1,0:T(8,128)(2,1)S(1)} %copy-done.24), channel_id=1, source_target_pairs={{8,16},{16,8},{9,17},{17,9},{10,18},{18,10},{11,19},{19,11},{12,20... | collective-permute-start | bytes 1179656 | tf_op jit(solution)/shard_map/ppermute | solution.py:629
  21.3 0.0 copy-start.21
  21.3 0.0 copy-start.22
  21.3 2.1 %collective-permute-start.5 = (bf16[144,1024]{1,0:T(8,128)(2,1)S(1)}, bf16[144,1024]{1,0:T(8,128)(2,1)S(1)}, u32[]{:S(2)}, u32[]{:S(2)}) collective-permute-start(bf16[144,1024]{1,0:T(8,128)(2,1)S(1)} %send_band.1), channel_id=1, source_target_pairs={{8,16},{16,8},{9,17},{17,9},{10,18},{18,10},{11,19},{19,11},{12,20... | collective-permute-start | bytes 884744 | tf_op jit(solution)/shard_map/ppermute | solution.py:629
  23.4 0.4 collective-permute-start.4
  23.8 4.1 %early_cross.1 = (f32[768,512]{1,0:T(8,128)S(1)}, f32[768,512]{1,0:T(8,128)S(1)}) custom-call(bf16[768,512]{1,0:T(8,128)(2,1)S(1)} %bitcast.15, bf16[48,1024]{1,0:T(8,128)(2,1)S(1)} %bitcast.10, bf16[512,48]{1,0:T(8,128)(2,1)S(1)} %copy-done.9), custom_call_target="tpu_custom_call" | custom-call | flops 5000000000 | bytes 4079616 | tf_op jit(solution)/shard_map/early_cross/pallas_call | solution.py:610
  27.9 0.0 copy-start.18
  28.0 1.2 %lon_strips.1 = (f32[384,512]{1,0:T(8,128)S(1)}, f32[384,512]{1,0:T(8,128)S(1)}) custom-call(bf16[768,512]{1,0:T(8,128)(2,1)S(1)} %bitcast.16, bf16[144,1024]{1,0:T(8,128)(2,1)S(1)} %collective-permute-done.2.f0_ref, bf16[144,1024]{1,0:T(8,128)(2,1)S(1)} %collective-permute-done.3.f1_ref, bf16[384,128]{1,0:T(8,128)(2,1)S(1)} %copy-done.21, ...), custom_call_target="tpu_custom_call" | custom-call | flops 1500000000 | bytes 3121152 | tf_op jit(solution)/shard_map/lon_strips/pallas_call | solution.py:610
  29.2 0.6 collective-permute-done.5.b1_ref
  29.9 0.0 copy-start.10
  29.9 0.0 copy-start.14
  29.9 0.0 copy-start.6
  29.9 0.0 copy-start.19
  29.9 0.0 copy-start.20
  29.9 1.3 %coarse.1.att_ref = bf16[80,512]{1,0:T(8,128)(2,1)S(1)} custom-call(bf16[48,512]{1,0:T(8,128)(2,1)S(1)} %bitcast.20, bf16[48,1024]{1,0:T(8,128)(2,1)S(1)} %bitcast.11, bf16[48,1024]{1,0:T(8,128)(2,1)S(1)} %collective-permute-done.c0_ref, bf16[48,1024]{1,0:T(8,128)(2,1)S(1)} %collective-permute-done.1.c1_ref, ...), custom_call_target="tpu_custom_call" | custom-call | flops 2000000000 | bytes 1167360 | tf_op jit(solution)/shard_map/coarse/pallas_call | solution.py:610
  31.3 0.4 send_late.1
  31.7 0.1 collective-permute-start.8
  31.8 0.0 copy-start.1
  31.8 0.0 copy-start.2
  31.8 0.0 copy-start.8
  31.8 0.0 copy-start.12
  31.8 0.0 copy-start.13
  31.9 4.1 %collective-permute-start.9 = (bf16[96,1024]{1,0:T(8,128)(2,1)S(1)}, bf16[96,1024]{1,0:T(8,128)(2,1)S(1)}, u32[]{:S(2)}, u32[]{:S(2)}) collective-permute-start(bf16[96,1024]{1,0:T(8,128)(2,1)S(1)} %get-tuple-element.56), channel_id=1, source_target_pairs={{8,16},{16,8},{9,17},{17,9},{10,18},{18,10},{11,19},{19,11},{12,20... | collective-permute-start | bytes 589832 | tf_op jit(solution)/shard_map/ppermute | solution.py:629
  36.0 3.4 %middle.1 = (f32[768,512]{1,0:T(8,128)S(1)}, f32[384,512]{1,0:T(8,128)S(1)}, f32[384,512]{1,0:T(8,128)S(1)}) custom-call(bf16[768,512]{1,0:T(8,128)(2,1)S(1)} %bitcast.17, f32[768,512]{1,0:T(8,128)S(1)} %get-tuple-element.42.oc_ref, f32[768,512]{1,0:T(8,128)S(1)} %get-tuple-element.43.lc_ref, bf16[48,1024]{1,0:T(8,128)(2,1)S(1)} %bitcast.12, ...), custom_call_target="tpu_custom_call" | custom-call | flops 5000000000 | bytes 9732096 | tf_op jit(solution)/shard_map/middle/pallas_call | solution.py:610
  39.5 25.7 %late.1 = bf16[768,512]{1,0:T(8,128)(2,1)} custom-call(bf16[768,512]{1,0:T(8,128)(2,1)S(1)} %bitcast.18, f32[768,512]{1,0:T(8,128)S(1)} %get-tuple-element.38.of_ref, f32[768,512]{1,0:T(8,128)S(1)} %get-tuple-element.39.lf_ref, f32[384,512]{1,0:T(8,128)S(1)} %get-tuple-element.46.om_ref, f32[384,512]{1,0:T(8,128)S(1)} %get-tuple-element.47.lm_ref, ...), custom_call_target="tpu_custom_call" | custom-call | flops 3000000000 | bytes 17317888 | tf_op jit(solution)/shard_map/late/pallas_call | solution.py:610
  (47 shorter events, 0.1 us)
Async XLA Ops:
  0.0 9.0 %copy-start.16 = (bf16[1536,128]{1,0:T(8,128)(2,1)S(1)}, bf16[1536,128]{1,0:T(8,128)(2,1)}, u32[]{:S(2)}) copy-start(bf16[1536,128]{1,0:T(8,128)(2,1)} %constant.46.clone.mask_ref) | copy-start | bytes 1179652
  0.0 9.0 %copy-start.17 = (bf16[768,128]{1,0:T(8,128)(2,1)S(1)}, bf16[768,128]{1,0:T(8,128)(2,1)}, u32[]{:S(2)}) copy-start(bf16[768,128]{1,0:T(8,128)(2,1)} %constant.45.clone.chosen_ref) | copy-start | bytes 589828
  0.0 9.0 %copy-start = (bf16[24,32,1024]{2,1,0:T(8,128)(2,1)S(1)}, bf16[24,32,1024]{2,1,0:T(8,128)(2,1)}, u32[]{:S(2)}) copy-start(bf16[24,32,1024]{2,1,0:T(8,128)(2,1)} %param.29) | copy-start | bytes 4718596
  3.5 10.2 %collective-permute-start = (bf16[48,1024]{1,0:T(8,128)(2,1)}, bf16[48,1024]{1,0:T(8,128)(2,1)S(1)}, u32[]{:S(2)}, u32[]{:S(2)}) collective-permute-start(bf16[48,1024]{1,0:T(8,128)(2,1)} %get-tuple-element.31), channel_id=1, source_target_pairs={{0,1},{2,3},{4,5},{6,7},{1,0},{3,2},{5,4},{7,6},{8,9},{10,11},{12,... | collective-permute-start | bytes 294920 | tf_op jit(solution)/shard_map/ppermute | solution.py:629
  3.8 17.4 %collective-permute-start.1 = (bf16[48,1024]{1,0:T(8,128)(2,1)}, bf16[48,1024]{1,0:T(8,128)(2,1)S(1)}, u32[]{:S(2)}, u32[]{:S(2)}) collective-permute-start(bf16[48,1024]{1,0:T(8,128)(2,1)} %get-tuple-element.32), channel_id=1, source_target_pairs={{1,2},{3,4},{5,6},{7,0},{2,1},{4,3},{6,5},{0,7},{9,10},{11,12},{13... | collective-permute-start | bytes 294920 | tf_op jit(solution)/shard_map/ppermute | solution.py:629
  6.1 17.3 %collective-permute-start.2 = (bf16[144,1024]{1,0:T(8,128)(2,1)}, bf16[144,1024]{1,0:T(8,128)(2,1)S(1)}, u32[]{:S(2)}, u32[]{:S(2)}) collective-permute-start(bf16[144,1024]{1,0:T(8,128)(2,1)} %get-tuple-element.40), channel_id=1, source_target_pairs={{0,1},{2,3},{4,5},{6,7},{1,0},{3,2},{5,4},{7,6},{8,9},{10,11},{12,... | collective-permute-start | bytes 884744 | tf_op jit(solution)/shard_map/ppermute | solution.py:629
  6.1 21.8 %collective-permute-start.3 = (bf16[144,1024]{1,0:T(8,128)(2,1)}, bf16[144,1024]{1,0:T(8,128)(2,1)S(1)}, u32[]{:S(2)}, u32[]{:S(2)}) collective-permute-start(bf16[144,1024]{1,0:T(8,128)(2,1)} %get-tuple-element.41), channel_id=1, source_target_pairs={{1,2},{3,4},{5,6},{7,0},{2,1},{4,3},{6,5},{0,7},{9,10},{11,12},{13... | collective-permute-start | bytes 884744 | tf_op jit(solution)/shard_map/ppermute | solution.py:629
  7.2 28.8 %collective-permute-start.6 = (bf16[192,1024]{1,0:T(8,128)(2,1)}, bf16[192,1024]{1,0:T(8,128)(2,1)S(1)}, u32[]{:S(2)}, u32[]{:S(2)}) collective-permute-start(bf16[192,1024]{1,0:T(8,128)(2,1)} %get-tuple-element.50), channel_id=1, source_target_pairs={{0,8},{16,24},{8,0},{24,16},{1,9},{17,25},{9,1},{25,17},{2,10},{18... | collective-permute-start | bytes 1179656 | tf_op jit(solution)/shard_map/ppermute | solution.py:629
  10.1 3.6 %copy-start.24 = (bf16[192,1024]{1,0:T(8,128)(2,1)S(1)}, bf16[192,1024]{1,0:T(8,128)(2,1)}, u32[]{:S(2)}) copy-start(bf16[192,1024]{1,0:T(8,128)(2,1)} %get-tuple-element.51) | copy-start | bytes 1179652
  10.1 11.1 %copy-start.3 = (bf16[6,8,1024]{2,1,0:T(8,128)(2,1)S(1)}, bf16[6,8,1024]{2,1,0:T(8,128)(2,1)}, u32[]{:S(2)}) copy-start(bf16[6,8,1024]{2,1,0:T(8,128)(2,1)} %param.31) | copy-start | bytes 294916
  10.1 13.7 %copy-start.5 = (bf16[24,32,512]{2,1,0:T(8,128)(2,1)S(1)}, bf16[24,32,512]{2,1,0:T(8,128)(2,1)}, u32[]{:S(2)}) copy-start(bf16[24,32,512]{2,1,0:T(8,128)(2,1)} %param.28) | copy-start | bytes 2359300
  10.1 13.7 %copy-start.9 = (bf16[512,48]{1,0:T(8,128)(2,1)S(1)}, bf16[512,48]{1,0:T(8,128)(2,1)}, u32[]{:S(2)}) copy-start(bf16[512,48]{1,0:T(8,128)(2,1)} %constant.47.clone.up_ref.early_hbm) | copy-start | bytes 147460
  13.7 22.2 %collective-permute-start.7 = (bf16[192,1024]{1,0:T(8,128)(2,1)S(1)}, bf16[192,1024]{1,0:T(8,128)(2,1)S(1)}, u32[]{:S(2)}, u32[]{:S(2)}) collective-permute-start(bf16[192,1024]{1,0:T(8,128)(2,1)S(1)} %copy-done.24), channel_id=1, source_target_pairs={{8,16},{16,8},{9,17},{17,9},{10,18},{18,10},{11,19},{19,11},{12,20... | collective-permute-start | bytes 1179656 | tf_op jit(solution)/shard_map/ppermute | solution.py:629
  21.3 6.6 %copy-start.21 = (bf16[384,128]{1,0:T(8,128)(2,1)S(1)}, bf16[384,128]{1,0:T(8,128)(2,1)}, u32[]{:S(2)}) copy-start(bf16[384,128]{1,0:T(8,128)(2,1)} %constant.48.clone.chosen_ref) | copy-start | bytes 294916
  21.3 6.6 %copy-start.22 = (bf16[288,128]{1,0:T(8,128)(2,1)S(1)}, bf16[288,128]{1,0:T(8,128)(2,1)}, u32[]{:S(2)}) copy-start(bf16[288,128]{1,0:T(8,128)(2,1)} %constant.49.clone.mask_ref) | copy-start | bytes 221188
  21.3 8.5 %collective-permute-start.5 = (bf16[144,1024]{1,0:T(8,128)(2,1)S(1)}, bf16[144,1024]{1,0:T(8,128)(2,1)S(1)}, u32[]{:S(2)}, u32[]{:S(2)}) collective-permute-start(bf16[144,1024]{1,0:T(8,128)(2,1)S(1)} %send_band.1), channel_id=1, source_target_pairs={{8,16},{16,8},{9,17},{17,9},{10,18},{18,10},{11,19},{19,11},{12,20... | collective-permute-start | bytes 884744 | tf_op jit(solution)/shard_map/ppermute | solution.py:629
  23.4 6.5 %collective-permute-start.4 = (bf16[144,1024]{1,0:T(8,128)(2,1)S(1)}, bf16[144,1024]{1,0:T(8,128)(2,1)S(1)}, u32[]{:S(2)}, u32[]{:S(2)}) collective-permute-start(bf16[144,1024]{1,0:T(8,128)(2,1)S(1)} %send_band.1), channel_id=1, source_target_pairs={{0,8},{16,24},{8,0},{24,16},{1,9},{17,25},{9,1},{25,17},{2,10},{18... | collective-permute-start | bytes 884744 | tf_op jit(solution)/shard_map/ppermute | solution.py:629
  27.9 1.9 %copy-start.15 = (bf16[6,8,512]{2,1,0:T(8,128)(2,1)S(1)}, bf16[6,8,512]{2,1,0:T(8,128)(2,1)}, u32[]{:S(2)}) copy-start(bf16[6,8,512]{2,1,0:T(8,128)(2,1)} %param.30) | copy-start | bytes 147460
  27.9 1.9 %copy-start.18 = (bf16[512,128]{1,0:T(8,128)(2,1)S(1)}, bf16[512,128]{1,0:T(8,128)(2,1)}, u32[]{:S(2)}) copy-start(bf16[512,128]{1,0:T(8,128)(2,1)} %constant.51.clone.mask_ref) | copy-start | bytes 393220
  27.9 1.9 %copy-start.23 = (bf16[80,128]{1,0:T(8,128)(2,1)S(1)}, bf16[80,128]{1,0:T(8,128)(2,1)}, u32[]{:S(2)}) copy-start(bf16[80,128]{1,0:T(8,128)(2,1)} %constant.50.clone.chosen_ref) | copy-start | bytes 61444
  29.9 1.4 %copy-start.10 = (bf16[192,144]{1,0:T(8,128)(2,1)S(1)}, bf16[192,144]{1,0:T(8,128)(2,1)}, u32[]{:S(2)}) copy-start(bf16[192,144]{1,0:T(8,128)(2,1)} %constant.53.clone.pr_ref) | copy-start | bytes 165892
  29.9 6.1 %copy-start.6 = (bf16[3,256,512]{2,1,0:T(8,128)(2,1)S(1)}, bf16[3,256,512]{2,1,0:T(8,128)(2,1)}, u32[]{:S(2)}) copy-start(bf16[3,256,512]{2,1,0:T(8,128)(2,1)} %constant.57.clone.late_ref.late_hbm) | copy-start | bytes 2359300
  29.9 6.1 %copy-start.19 = (bf16[384,128]{1,0:T(8,128)(2,1)S(1)}, bf16[384,128]{1,0:T(8,128)(2,1)}, u32[]{:S(2)}) copy-start(bf16[384,128]{1,0:T(8,128)(2,1)} %constant.56.clone.mask_ref) | copy-start | bytes 294916
  29.9 6.1 %copy-start.20 = (bf16[384,128]{1,0:T(8,128)(2,1)S(1)}, bf16[384,128]{1,0:T(8,128)(2,1)}, u32[]{:S(2)}) copy-start(bf16[384,128]{1,0:T(8,128)(2,1)} %constant.55.clone.chosen_ref) | copy-start | bytes 294916
  31.7 7.7 %collective-permute-start.8 = (bf16[96,1024]{1,0:T(8,128)(2,1)S(1)}, bf16[96,1024]{1,0:T(8,128)(2,1)S(1)}, u32[]{:S(2)}, u32[]{:S(2)}) collective-permute-start(bf16[96,1024]{1,0:T(8,128)(2,1)S(1)} %get-tuple-element.55), channel_id=1, source_target_pairs={{0,8},{16,24},{8,0},{24,16},{1,9},{17,25},{9,1},{25,17},{2,10},{18... | collective-permute-start | bytes 589832 | tf_op jit(solution)/shard_map/ppermute | solution.py:629
  31.8 7.6 %copy-start.1 = (bf16[4896,128]{1,0:T(8,128)(2,1)S(1)}, bf16[4896,128]{1,0:T(8,128)(2,1)}, u32[]{:S(2)}) copy-start(bf16[4896,128]{1,0:T(8,128)(2,1)} %constant.59.clone.exact_mask_hbm) | copy-start | bytes 3760132
  31.8 7.6 %copy-start.2 = (bf16[3,768,144]{2,1,0:T(8,128)(2,1)S(1)}, bf16[3,768,144]{2,1,0:T(8,128)(2,1)}, u32[]{:S(2)}) copy-start(bf16[3,768,144]{2,1,0:T(8,128)(2,1)} %constant.62.clone.up_ref) | copy-start | bytes 1990660
  31.8 7.6 %copy-start.7 = (bf16[512,512]{1,0:T(8,128)(2,1)S(1)}, bf16[512,512]{1,0:T(8,128)(2,1)}, u32[]{:S(2)}) copy-start(bf16[512,512]{1,0:T(8,128)(2,1)} %weight_ref.1) | copy-start | bytes 1572868
  31.8 7.6 %copy-start.8 = (bf16[768,128]{1,0:T(8,128)(2,1)S(1)}, bf16[768,128]{1,0:T(8,128)(2,1)}, u32[]{:S(2)}) copy-start(bf16[768,128]{1,0:T(8,128)(2,1)} %constant.58.clone.exact_chosen_hbm) | copy-start | bytes 589828
  31.8 7.6 %copy-start.12 = (bf16[192,128]{1,0:T(8,128)(2,1)S(1)}, bf16[192,128]{1,0:T(8,128)(2,1)}, u32[]{:S(2)}) copy-start(bf16[192,128]{1,0:T(8,128)(2,1)} %constant.61.clone.mask_ref) | copy-start | bytes 147460
  31.8 7.6 %copy-start.13 = (bf16[192,128]{1,0:T(8,128)(2,1)S(1)}, bf16[192,128]{1,0:T(8,128)(2,1)}, u32[]{:S(2)}) copy-start(bf16[192,128]{1,0:T(8,128)(2,1)} %constant.60.clone.chosen_ref) | copy-start | bytes 147460
  31.9 7.6 %collective-permute-start.9 = (bf16[96,1024]{1,0:T(8,128)(2,1)S(1)}, bf16[96,1024]{1,0:T(8,128)(2,1)S(1)}, u32[]{:S(2)}, u32[]{:S(2)}) collective-permute-start(bf16[96,1024]{1,0:T(8,128)(2,1)S(1)} %get-tuple-element.56), channel_id=1, source_target_pairs={{8,16},{16,8},{9,17},{17,9},{10,18},{18,10},{11,19},{19,11},{12,20... | collective-permute-start | bytes 589832 | tf_op jit(solution)/shard_map/ppermute | solution.py:629
  (3 other events, 3.8 us)
